TPU v7x, 256 devices: a whole 4x4x8 slice. The times are simulated.
256 devices in a mesh: pat: 16 (over z, core), pb: 16 (over x, y).
Axes of the slice: x: 4, y: 4, z: 8, core: 2. Of those that a mesh axis runs over, the one named last changes fastest.
Arguments:
- measured: float32 [32768, 4096], P(('pat', 'pb')), may hold values from 1 to 10
- resolution: float32 [33, 4096], replicated, may hold values from 0.05 to 1
- loadings_start: float32 [32768, 128], P('pat'), may hold values from 0.05 to 0.5
- components_start: float32 [128, 4096], P(None, 'pb'), may hold values from 0.05 to 0.5
Outputs:
- loadings: float32 [32768, 128], P('pat')
- components: float32 [128, 4096], P(None, 'pb')
All inputs are finite; a program needn't handle non-finite values.
Results may differ from a plain program's by a relative error of at most 0.00013.
Values sent between devices are 32-bit elements; how exact they have to be, the bound alone decides.
No kernel may reach another device: no remote copies, remote signals or barrier semaphores. Data moves between devices by JAX's collectives and lax.ppermute only.
A program may use at most 128 MiB of HBM per device.

v0:
```python
import jax
import jax.numpy as jnp
from jax import lax
from jax.sharding import PartitionSpec as P

RADIUS = 16
ITERS = 3


def smear_forward(field, resolution):
    width = field.shape[1]
    padded = jnp.pad(field, ((0, 0), (RADIUS, RADIUS)))
    total = jnp.zeros(field.shape, jnp.float32)
    for offset in range(2 * RADIUS + 1):
        total = total + resolution[offset][None, :] * padded[:, offset : offset + width]
    return total


def smear_back(field, resolution):
    width = field.shape[1]
    total = jnp.zeros(field.shape, jnp.float32)
    for offset in range(2 * RADIUS + 1):
        weighted = jnp.pad(resolution[offset][None, :] * field, ((0, 0), (RADIUS, RADIUS)))
        begin = 2 * RADIUS - offset
        total = total + weighted[:, begin : begin + width]
    return total


def local(measured, resolution, loadings_start, components_start):
    high = lax.Precision.HIGHEST
    blurred = smear_forward(measured, resolution)
    back = smear_back(measured / blurred, resolution)
    weight_sum = smear_back(jnp.ones((1, measured.shape[1]), jnp.float32), resolution)
    corrected_rows = measured * back / weight_sum
    corrected = lax.all_to_all(corrected_rows, "pb", split_axis=1, concat_axis=0, tiled=True)
    loadings = loadings_start
    components = components_start
    for step in range(ITERS):
        quotient = corrected / jnp.dot(loadings, components, precision=high)
        numerator = jnp.dot(loadings.T, quotient, precision=high)
        w_totals = jnp.sum(loadings, axis=0)
        numerator, w_totals = lax.psum((numerator, w_totals), "pat")
        components = components * numerator / w_totals[:, None]
        quotient = corrected / jnp.dot(loadings, components, precision=high)
        w_numer = jnp.dot(quotient, components.T, precision=high)
        w_numer, h_totals = lax.psum((w_numer, jnp.sum(components, axis=1)), "pb")
        loadings = loadings * w_numer / h_totals[None, :]
    return (loadings, components)


def solution(mesh):
    return jax.shard_map(
        local,
        mesh=mesh,
        in_specs=(P(("pat", "pb"), None), P(), P("pat", None), P(None, "pb")),
        out_specs=(P("pat", None), P(None, "pb")),
        check_vma=False,
    )
```

profile of v0, /device:TPU:32, one launch (start us, length us, event | category | flops | bytes accessed | tf_op | source)
XLA Modules:
  0.0 795.1 jit_solution(184189251099669806)
XLA Ops:
  7.2 2.2 fusion.90
  9.4 2.7 fusion.89
  12.1 1.9 copy.17
  14.0 2.1 fusion.83
  16.2 22.0 %broadcast_multiply_fusion.31 = (f32[128,4096]{0,1:T(8,128)}, f32[128,4096]{0,1:T(8,128)S(1)}) fusion(f32[4096]{0:T(1024)S(1)} %bitcast.137, f32[128,4096]{0,1:T(8,128)S(1)} %copy.17, f32[4096]{0:T(1024)S(1)} %bitcast.133, f32[4096]{0:T(1024)S(1)} %bitcast.75, f32[4096]{0:T(1024)S(1)} %bitcast.79, f32[4096]{0:T(1024)S(1)} %bitcast.81, ...), kind=kLoop, calls=%fused_computation.135 | loop fusion | flops 35127296 | bytes 6832128 | tf_op jit(solution)/shard_map/mul | solution.py:23
  38.2 10.9 %broadcast_multiply_fusion.29 = (f32[128,4096]{0,1:T(8,128)S(1)}, f32[128,4096]{0,1:T(8,128)S(1)}, f32[128,4096]{0,1:T(8,128)S(1)}, f32[128,4096]{0,1:T(8,128)S(...) fusion(f32[128,4096]{0,1:T(8,128)S(1)} %get-tuple-element.19, ...), kind=kLoop, calls=%fused_computation.133 | loop fusion | flops 6815744 | bytes 29573120 | tf_op jit(solution)/shard_map/mul | solution.py:23
  49.1 14.6 %broadcast_multiply_fusion.30 = (f32[128,4096]{0,1:T(8,128)}, f32[128,4096]{0,1:T(8,128)}, f32[128,4096]{0,1:T(8,128)}, f32[128,4096]{0,1:T(8,128)}, f32[128,409...) fusion(f32[128,4096]{0,1:T(8,128)S(1)} %get-tuple-element.19, ...), kind=kLoop, calls=%fused_computation.134 | loop fusion | flops 9437184 | bytes 40140800 | tf_op jit(solution)/shard_map/mul | solution.py:23
  63.7 20.0 %fusion.34 = f32[128,4096]{0,1:T(8,128)} fusion(f32[128,4096]{0,1:T(8,128)S(1)} %copy.17, f32[128,4096]{0,1:T(8,128)} %get-tuple-element.27, f32[128,4096]{0,1:T(8,128)} %get-tuple-element.26, f32[128,4096]{0,1:T(8,128)} %get-tuple-element.25, f32[128,4096]{0,1:T(8,128)} %get-tuple-element.24, f32[128,4096]{0,1:T(8,128)} %get-tuple-element.23, ...), kind=kLoop, calls=%fused_computation.72 | loop fusion | flops 18350080 | bytes 73433088 | tf_op jit(solution)/shard_map/div | solution.py:34
  83.8 35.6 %all_to_all.19 = f32[128,16,256]{0,2,1:T(8,128)} all-to-all(f32[128,16,256]{0,2,1:T(8,128)} %bitcast.67), channel_id=1, replica_groups=mesh['pat'=16,'pb'=16] {'pb'}, dimensions={1} | all-to-all | bytes 4194304 | tf_op jit(solution)/shard_map/all_to_all | solution.py:35
  119.4 3.0 copy.18
  122.4 3.5 convolution_divide_fusion.4
  125.9 4.2 convolution_bitcast_fusion.1
  130.1 0.0 all-reduce.74.cloned.1.call-start
  130.1 0.1 copy.19
  130.2 0.3 reduce_sum.54
  130.5 23.4 %psum.85 = f32[128]{0:T(128)S(1)} all-reduce(f32[128]{0:T(128)S(1)} %reduce_sum.54), channel_id=1, replica_groups=mesh['pat'=16,'pb'=16] {'pat'}, use_global_device_ids=true, to_apply=%region_2.3 | all-reduce | flops 128 | bytes 1024 | tf_op jit(solution)/shard_map/psum | solution.py:42
  154.0 2.9 copy.20
  156.9 77.8 %all-reduce.72.cloned.1.call-done = f32[128,256]{0,1:T(8,128)} async-done(((f32[128,256]{0,1:T(8,128)}), f32[128,256]{0,1:T(8,128)}) %all-reduce.72.cloned.1.call-update) | async-done | bytes 131088 | tf_op jit(solution)/shard_map/psum | solution.py:42
  234.6 1.0 fusion.88
  235.6 3.5 fusion
  239.1 4.5 fusion.91
  243.7 40.5 %psum.87 = f32[128]{0:T(128)S(1)} all-reduce(f32[128]{0:T(128)S(1)} %get-tuple-element.16), channel_id=1, replica_groups=mesh['pat'=16,'pb'=16] {'pb'}, use_global_device_ids=true, to_apply=%region_5.6 | all-reduce | flops 128 | bytes 1024 | tf_op jit(solution)/shard_map/psum | solution.py:46
  284.2 59.6 %all-reduce.74.cloned.1.call-done = f32[2048,128]{1,0:T(8,128)} async-done(((f32[2048,128]{1,0:T(8,128)}), f32[2048,128]{1,0:T(8,128)}) %all-reduce.74.cloned.1.call-update) | async-done | bytes 1048592 | tf_op jit(solution)/shard_map/psum | solution.py:46
  343.8 1.5 fusion.87
  345.4 3.4 convolution_divide_fusion.3
  348.8 4.1 fusion.92
  352.9 0.0 all-reduce.78.cloned.1.call-start
  353.0 21.8 %psum.89 = f32[128]{0:T(128)S(1)} all-reduce(f32[128]{0:T(128)S(1)} %get-tuple-element.14), channel_id=1, replica_groups=mesh['pat'=16,'pb'=16] {'pat'}, use_global_device_ids=true, to_apply=%region_8.9 | all-reduce | flops 128 | bytes 1024 | tf_op jit(solution)/shard_map/psum | solution.py:42
  374.8 82.4 %all-reduce.76.cloned.1.call-done = f32[128,256]{0,1:T(8,128)} async-done(((f32[128,256]{0,1:T(8,128)}), f32[128,256]{0,1:T(8,128)}) %all-reduce.76.cloned.1.call-update) | async-done | bytes 131088 | tf_op jit(solution)/shard_map/psum | solution.py:42
  457.3 1.0 fusion.86
  458.2 3.4 convolution_divide_fusion.2
  461.6 2.8 fusion.93
  464.4 0.0 all-reduce.80.cloned.1.call-start
  464.5 40.6 %psum.91 = f32[128]{0:T(128)S(1)} all-reduce(f32[128]{0:T(128)S(1)} %get-tuple-element.12), channel_id=1, replica_groups=mesh['pat'=16,'pb'=16] {'pb'}, use_global_device_ids=true, to_apply=%region_11.12 | all-reduce | flops 128 | bytes 1024 | tf_op jit(solution)/shard_map/psum | solution.py:46
  505.1 59.6 %all-reduce.78.cloned.1.call-done = f32[2048,128]{1,0:T(8,128)} async-done(((f32[2048,128]{1,0:T(8,128)}), f32[2048,128]{1,0:T(8,128)}) %all-reduce.78.cloned.1.call-update) | async-done | bytes 1048592 | tf_op jit(solution)/shard_map/psum | solution.py:46
  564.7 1.5 fusion.85
  566.2 3.4 convolution_divide_fusion.1
  569.6 4.1 fusion.94
  573.8 0.0 all-reduce.82.cloned.1.call-start
  573.8 21.8 %psum.93 = f32[128]{0:T(128)S(1)} all-reduce(f32[128]{0:T(128)S(1)} %get-tuple-element.10), channel_id=1, replica_groups=mesh['pat'=16,'pb'=16] {'pat'}, use_global_device_ids=true, to_apply=%region_14.15 | all-reduce | flops 128 | bytes 1024 | tf_op jit(solution)/shard_map/psum | solution.py:42
  595.7 82.5 %all-reduce.80.cloned.1.call-done = f32[128,256]{0,1:T(8,128)} async-done(((f32[128,256]{0,1:T(8,128)}), f32[128,256]{0,1:T(8,128)}) %all-reduce.80.cloned.1.call-update) | async-done | bytes 131088 | tf_op jit(solution)/shard_map/psum | solution.py:42
  678.1 1.0 fusion.84
  679.1 3.4 convolution_divide_fusion
  682.5 2.8 fusion.95
  685.3 0.8 copy.23
  686.1 40.4 %psum.95 = f32[128]{0:T(128)S(1)} all-reduce(f32[128]{0:T(128)S(1)} %get-tuple-element.8), channel_id=1, replica_groups=mesh['pat'=16,'pb'=16] {'pb'}, use_global_device_ids=true, to_apply=%region_17.18 | all-reduce | flops 128 | bytes 1024 | tf_op jit(solution)/shard_map/psum | solution.py:46
  726.5 59.1 %all-reduce.82.cloned.1.call-done = f32[2048,128]{1,0:T(8,128)} async-done(((f32[2048,128]{1,0:T(8,128)}), f32[2048,128]{1,0:T(8,128)}) %all-reduce.82.cloned.1.call-update) | async-done | bytes 1048592 | tf_op jit(solution)/shard_map/psum | solution.py:46
  785.5 2.3 multiply_divide_fusion
  (12 shorter events, 0.2 us)
Async XLA Ops:
  7.2 227.5 %all-reduce.72.cloned.1.call-start = ((), (), s32[]{:S(2)}) async-start(), calls=%async_computation.1 | async-start | bytes 262144 | tf_op jit(solution)/shard_map/psum | solution.py:42
  119.3 3.0 copy-start
  119.4 3.0 copy-start.1
  130.1 213.7 %all-reduce.74.cloned.1.call-start = ((), (), s32[]{:S(2)}) async-start(), calls=%async_computation.2 | async-start | bytes 2097152 | tf_op jit(solution)/shard_map/psum | solution.py:46
  243.6 213.6 %all-reduce.76.cloned.1.call-start = ((), (), s32[]{:S(2)}) async-start(), calls=%async_computation.3 | async-start | bytes 262144 | tf_op jit(solution)/shard_map/psum | solution.py:42
  352.9 211.7 %all-reduce.78.cloned.1.call-start = ((), (), s32[]{:S(2)}) async-start(), calls=%async_computation.4 | async-start | bytes 2097152 | tf_op jit(solution)/shard_map/psum | solution.py:46
  464.4 213.7 %all-reduce.80.cloned.1.call-start = ((), (), s32[]{:S(2)}) async-start(), calls=%async_computation.5 | async-start | bytes 262144 | tf_op jit(solution)/shard_map/psum | solution.py:42
  573.8 211.8 %all-reduce.82.cloned.1.call-start = ((), (), s32[]{:S(2)}) async-start(), calls=%async_computation.6 | async-start | bytes 2097152 | tf_op jit(solution)/shard_map/psum | solution.py:46
Sparse Core Ops, SparseCore 0:
  130.2 104.3 all-reduce.71
  243.8 100.0 all-reduce.73
  353.1 104.1 all-reduce.75
  464.6 100.0 all-reduce.77
  573.9 104.2 all-reduce.79
  685.4 100.0 all-reduce.81
where the time goes:
time: 801 us; the launch traced here: 795 us
  waiting for transfers between devices  421 us (53%)
  blocking collectives  224 us (28%)
  other arithmetic  78.2 us (10%)
  matrix products  43.2 us (5%)
  between operations  14.7 us (2%)
  local copies, waits for them, and re-layouts  13.6 us (2%)
    psum x3, waiting for transfers between devices, local(): numerator, w_totals = lax.psum((numerator, w_totals), 'pat')  243 us
    psum x3, waiting for transfers between devices, local(): w_numer, h_totals = lax.psum((w_numer, jnp.sum(components, axis=1)), 'pb')  178 us
    psum x3, blocking collectives, local(): w_numer, h_totals = lax.psum((w_numer, jnp.sum(components, axis=1)), 'pb')  122 us
    psum x3, blocking collectives, local(): numerator, w_totals = lax.psum((numerator, w_totals), 'pat')  67.1 us
    mul x3, other arithmetic, smear_back(): resolution[offset][None, :] * field  47.6 us
    all_to_all x1, blocking collectives, local(): lax.all_to_all(corrected_rows, 'pb', split_axis=1, concat_axis=0, tiled=T...  35.6 us
    dot_general x6, matrix products, local(): quotient = corrected / jnp.dot(loadings, components, precision=high)  20.7 us
    div x1, other arithmetic, local(): corrected_rows = measured * back / weight_sum  20 us
  transfers between devices with their start and end apart: 6, of which 6 were waited for; matrix products, arithmetic and copies ran while one was open for 1% of the time, Pallas kernels for 0%

commit v1 on v0

v1 whole, which is shorter than its diff:
```python
import functools
import jax
import jax.numpy as jnp
from jax import lax
from jax.experimental import pallas as pl
from jax.experimental.pallas import tpu as pltpu
from jax.sharding import Mesh, PartitionSpec as P

RADIUS = 16
TAPS = 33
ITERS = 3
LANES = 128
VMEM = pltpu.MemorySpace.VMEM
SMEM = pltpu.MemorySpace.SMEM
F32 = jnp.float32
BF16 = jnp.bfloat16


def split(x):
    hi = x.astype(BF16)
    return hi, (x - hi.astype(F32)).astype(BF16)


def mm(a, b, dims):
    return lax.dot_general(a, b, (dims, ((), ())), preferred_element_type=F32)


def mm3(a, b, dims):
    (ah, al), (bh, bl) = a, b
    return mm(ah, bh, dims) + (mm(al, bh, dims) + mm(ah, bl, dims))


NT = ((1,), (1,))
NN = ((1,), (0,))


def smear_kernel(blocks, idx_ref, field_ref, res_ref, o0, o1, o2, o3, vh, vl, uh, ul, ch, cl, hh, hl, pad):
    rows = field_ref.shape[0]
    xi, ci = idx_ref[0], idx_ref[1]
    zero = jnp.zeros((rows, LANES), BF16)
    for ref in (vh, vl, uh, ul):
        ref[:, 0:LANES] = zero
        ref[:, (blocks + 1) * LANES : (blocks + 2) * LANES] = zero
    zero = jnp.zeros((LANES, LANES), BF16)
    for ref in (ch, cl, hh, hl):
        ref[0:LANES, :] = zero
        ref[(blocks + 1) * LANES : (blocks + 2) * LANES, :] = zero
    pad[...] = jnp.zeros((LANES, LANES), F32)
    near = lax.broadcasted_iota(jnp.int32, (rows, LANES), 1) < LANES // 2
    row = lax.broadcasted_iota(jnp.int32, (LANES, LANES), 0)
    col = lax.broadcasted_iota(jnp.int32, (LANES, LANES), 1)
    inside = jnp.abs(row - col) <= RADIUS

    def at(j):
        return pl.ds(pl.multiple_of((j + 1) * LANES, LANES), LANES)

    def window(ref, j):
        halo = jnp.where(near, ref[:, at(j + 1)], ref[:, at(j - 1)])
        return jnp.concatenate([ref[:, at(j)], halo], axis=1)

    def prepare(j, _):
        cols = pl.ds(pl.multiple_of(j * LANES, LANES), LANES)
        h, l = split(field_ref[:, cols])
        vh[:, at(j)] = h
        vl[:, at(j)] = l
        pad[0:TAPS, :] = res_ref[:, cols]
        band = pltpu.roll(jnp.transpose(pad[...]), LANES - RADIUS, 1, stride=1, stride_axis=0)
        h, l = split(jnp.where(inside, band, 0.0))
        ch[at(j), :] = h
        cl[at(j), :] = l
        h, l = split(jnp.where(inside, 0.0, band))
        hh[at(j), :] = h
        hl[at(j), :] = l
        return _

    lax.fori_loop(0, blocks, prepare, 0, unroll=2)

    def forward(j, _):
        cols = pl.ds(pl.multiple_of(j * LANES, LANES), LANES)
        bh = jnp.concatenate([ch[at(j), :], hh[at(j), :]], axis=1)
        bl = jnp.concatenate([cl[at(j), :], hl[at(j), :]], axis=1)
        blurred = mm3((window(vh, j), window(vl, j)), (bh, bl), NT)
        h, l = split(field_ref[:, cols] / blurred)
        uh[:, at(j)] = h
        ul[:, at(j)] = l
        return _

    lax.fori_loop(0, blocks, forward, 0, unroll=4)

    def stack(c, h, j):
        half = LANES // 2
        after = h[pl.ds(pl.multiple_of((j + 2) * LANES, LANES), half), :]
        before = h[pl.ds(pl.multiple_of(j * LANES + half, half), half), :]
        return jnp.concatenate([c[at(j), :], after, before], axis=0)

    per = blocks // 4
    for d, out in enumerate((o0, o1, o2, o3)):
        def back(i, _):
            j = (xi ^ d) * per + (i ^ (ci * (per // 2)))
            bh = stack(ch, hh, j)
            bl = stack(cl, hl, j)
            total = mm3((window(uh, j), window(ul, j)), (bh, bl), NN)
            weight = jnp.sum(bh.astype(F32) + bl.astype(F32), axis=0, keepdims=True)
            v = field_ref[:, pl.ds(pl.multiple_of(j * LANES, LANES), LANES)]
            out[:, pl.ds(pl.multiple_of(i * LANES, LANES), LANES)] = v * total / weight
            return _

        lax.fori_loop(0, per, back, 0, unroll=4)


def whole(n, space=VMEM):
    return [pl.BlockSpec(memory_space=space)] * n


def smear(idx, field, resolution):
    rows, width = field.shape
    blocks = width // LANES
    padded = (blocks + 2) * LANES
    return pl.pallas_call(
        functools.partial(smear_kernel, blocks),
        out_shape=[jax.ShapeDtypeStruct((rows, width // 4), F32)] * 4,
        in_specs=whole(1, SMEM) + whole(2),
        out_specs=whole(4),
        scratch_shapes=[pltpu.VMEM((rows, padded), BF16)] * 4
        + [pltpu.VMEM((padded, LANES), BF16)] * 4
        + [pltpu.VMEM((LANES, LANES), F32)],
        compiler_params=pltpu.CompilerParams(vmem_limit_bytes=48 << 20),
        name="smear",
    )(idx, field, resolution)


def fold(x):
    return jnp.sum(x.reshape(x.shape[0] // 8, 8, x.shape[1]), axis=0)


def components_kernel(x0, x1, x2, x3, l0, l1, l2, l3, ha, hb, keep, send):
    loads = jnp.concatenate([l0[...], l1[...], l2[...], l3[...]], axis=0)
    pair = split(loads)
    pair_t = split(jnp.transpose(loads))
    sums = fold(loads)
    half = ha.shape[0]
    tile = 256
    for h_ref, out, base in ((hb, send, half), (ha, keep, 0)):
        for t in range(half // tile):
            h = split(h_ref[t * tile : (t + 1) * tile, :])
            cols = slice(base + t * tile, base + (t + 1) * tile)
            x = jnp.concatenate([r[:, cols] for r in (x0, x1, x2, x3)], axis=0)
            quotient = split(x / mm3(pair, h, NT))
            out[t * tile : (t + 1) * tile, :] = jnp.transpose(mm3(pair_t, quotient, NN))
        out[half : half + 8, :] = sums


def components_part(xs, ls, ha, hb):
    half, comps = ha.shape
    return pl.pallas_call(
        components_kernel,
        out_shape=[jax.ShapeDtypeStruct((half + 8, comps), F32)] * 2,
        in_specs=whole(10),
        out_specs=whole(2),
        compiler_params=pltpu.CompilerParams(vmem_limit_bytes=48 << 20),
        name="components_part",
    )(*xs, *ls, ha, hb)


def loadings_kernel(x0, x1, x2, x3, l0, l1, l2, l3, ha, hb, o0, o1, o2, o3):
    h = jnp.concatenate([ha[...], hb[...]], axis=0)
    pair = split(h)
    sums = fold(h)
    for x, l, out in zip((x0, x1, x2, x3), (l0, l1, l2, l3), (o0, o1, o2, o3)):
        rows = x.shape[0]
        quotient = split(x[...] / mm3(split(l[...]), pair, NT))
        out[0:rows, :] = mm3(quotient, pair, NN)
        out[rows : rows + 8, :] = sums


def loadings_part(xs, ls, ha, hb):
    rows, comps = ls[0].shape
    return pl.pallas_call(
        loadings_kernel,
        out_shape=[jax.ShapeDtypeStruct((rows + 8, comps), F32)] * 4,
        in_specs=whole(10),
        out_specs=whole(4),
        compiler_params=pltpu.CompilerParams(vmem_limit_bytes=48 << 20),
        name="loadings_part",
    )(*xs, *ls, ha, hb)


SPLIT = ("z", "c", "x", "y")


def swap(x, axis, distance):
    size = 2 if axis == "c" else 4
    return lax.ppermute(x, axis, [(i, i ^ distance) for i in range(size)])


def spread(x, axes, copies):
    y = jnp.broadcast_to(x[None], (copies,) + x.shape)
    return lax.all_to_all(y, axes, 0, 0).reshape((-1,) + x.shape[1:])


def local(measured, resolution, loadings_start, components_start):
    xi, yi, ci = lax.axis_index("x"), lax.axis_index("y"), lax.axis_index("c")
    zi = lax.axis_index("z")
    comps = components_start.shape[0]
    start = spread(components_start.T, "y", 4)
    half = start.shape[0] // 2
    mine = lax.dynamic_slice_in_dim(start, ci * half, half)
    theirs = lax.dynamic_slice_in_dim(start, (1 - ci) * half, half)
    idx = jnp.stack([xi, ci]).astype(jnp.int32)
    chunks = smear(idx, measured, resolution)
    xs = [chunks[0]] + [swap(chunks[d], "x", d) for d in (1, 2, 3)]
    rows = measured.shape[0]
    ls = [lax.dynamic_slice_in_dim(loadings_start, ((xi ^ d) * 4 + yi) * rows, rows) for d in range(4)]
    group = 32
    part = half // group
    piece = lax.dynamic_slice_in_dim(mine, (zi * 4 + yi) * part, part)
    for step in range(ITERS):
        keep, send = components_part(xs, ls, mine, theirs)
        both = keep + swap(send, "c", 1)
        packed = jnp.concatenate(
            [both[:half].reshape(group, part, comps), jnp.broadcast_to(both[half:][None], (group, 8, comps))], axis=1
        )
        total = jnp.sum(lax.all_to_all(packed, ("z", "y"), 0, 0), axis=0)
        piece = piece * total[:part] / jnp.sum(total[part:], axis=0, keepdims=True)
        mine = spread(piece, ("z", "y"), group)
        theirs = swap(mine, "c", 1)
        parts = loadings_part(xs, ls, mine, theirs)
        total = parts[0] + swap(parts[1], "x", 1) + swap(parts[2], "x", 2) + swap(parts[3], "x", 3)
        own = ls[0] * total[:rows] / jnp.sum(total[rows:], axis=0, keepdims=True)
        if step < ITERS - 1:
            ls = [own] + [swap(own, "x", d) for d in (1, 2, 3)]
    loadings = spread(own, ("x", "y"), 16)
    low = lax.dynamic_slice_in_dim(mine, (yi % 2) * (half // 2), half // 2)
    high = lax.dynamic_slice_in_dim(theirs, (yi % 2) * (half // 2), half // 2)
    components = jnp.where(yi // 2 == ci, low, high).T
    return (loadings, components)


def solution(mesh):
    inner = Mesh(mesh.devices.reshape(8, 2, 4, 4), SPLIT)
    return jax.shard_map(
        local,
        mesh=inner,
        in_specs=(P(SPLIT, None), P(), P(("z", "c"), None), P(None, ("x", "y"))),
        out_specs=(P(("z", "c"), None), P(None, ("x", "y"))),
        check_vma=False,
    )
```

time: 801 us -> 249 us (0.31)
  waiting for transfers between devices: 421 us -> 75 us
  blocking collectives: 224 us -> 87.1 us
  other arithmetic: 78.2 us -> 2.12 us
  starting transfers between devices: 0.25 us -> 47.8 us
  matrix products: 43.2 us -> 0 us
  Pallas kernels: 0 us -> 26.4 us
  between operations: 14.7 us -> 0.98 us
    psum x6 -> x0, waiting for transfers between devices: 421 us -> none  [the longest x3 243 us: local(): numerator, w_totals = lax.psum((numerator, w_totals), 'pat')]
    psum x6 -> x0, blocking collectives: 189 us -> none  [the longest x3 122 us: local(): w_numer, h_totals = lax.psum((w_numer, jnp.sum(components, axis=1)), 'pb')]
    all_to_all x1 -> x5, blocking collectives: 35.6 us -> 87.1 us  [the longest x3 48.2 us: spread(): return lax.all_to_all(y, axes, 0, 0).reshape((-1,) + x.shape[1:])]
    mul x3 -> x0, other arithmetic: 47.6 us -> none  [smear_back(): resolution[offset][None, :] * field]
    dot_general x12 -> x0, matrix products: 43.2 us -> none  [the longest x6 20.7 us: local(): quotient = corrected / jnp.dot(loadings, components, precision=high)]
    all_to_all x0 -> x3, waiting for transfers between devices: none -> 38 us  [the longest x2 23.1 us: spread(): return lax.all_to_all(y, axes, 0, 0).reshape((-1,) + x.shape[1:])]
    ppermute x0 -> x24, waiting for transfers between devices: none -> 37 us  [swap(): return lax.ppermute(x, axis, [(i, i ^ distance) for i in range(size)])]
    ppermute x0 -> x24, starting transfers between devices: none -> 27.9 us  [swap(): return lax.ppermute(x, axis, [(i, i ^ distance) for i in range(size)])]
  transfers between devices with their start and end apart: 6 -> 27, of which waited for: 6 -> 22; matrix products, arithmetic and copies ran while one was open for 1% -> 2% of each run, Pallas kernels for 0% -> 0%
where the time goes in v1:
time: 249 us; the launch traced here: 248 us
  blocking collectives  87.1 us (35%)
  waiting for transfers between devices  75 us (30%)
  starting transfers between devices  47.8 us (19%)
  Pallas kernels  26.4 us (11%)
  local copies, waits for them, and re-layouts  8.58 us (3%)
    all_to_all x3, blocking collectives, spread(): return lax.all_to_all(y, axes, 0, 0).reshape((-1,) + x.shape[1:])  48.2 us
    all_to_all x2, blocking collectives, local(): total = jnp.sum(lax.all_to_all(packed, ('z', 'y'), 0, 0), axis=0)  38.9 us
    ppermute x24, waiting for transfers between devices, swap(): return lax.ppermute(x, axis, [(i, i ^ distance) for i in range(size)])  37 us
    ppermute x24, starting transfers between devices, swap(): return lax.ppermute(x, axis, [(i, i ^ distance) for i in range(size)])  27.9 us
    all_to_all x2, waiting for transfers between devices, spread(): return lax.all_to_all(y, axes, 0, 0).reshape((-1,) + x.shape[1:])  23.1 us
    all_to_all x1, waiting for transfers between devices, local(): total = jnp.sum(lax.all_to_all(packed, ('z', 'y'), 0, 0), axis=0)  15 us
    all_to_all x1, starting transfers between devices, local(): total = jnp.sum(lax.all_to_all(packed, ('z', 'y'), 0, 0), axis=0)  11.4 us
    pallas_call x1, Pallas kernels, smear(): pl.pallas_call(functools.partial(smear_kernel, blocks), out_shape=[jax.Sh...  10.7 us
  transfers between devices with their start and end apart: 27, of which 22 were waited for; matrix products, arithmetic and copies ran while one was open for 2% of the time, Pallas kernels for 0%

profile of v1, /device:TPU:32, one launch (start us, length us, event | category | flops | bytes accessed | tf_op | source)
XLA Modules:
  0.0 248.0 jit_solution(29558880465945896)
XLA Ops:
  0.7 1.6 copy-done
  3.4 10.7 %smear.1 = (f32[128,1024]{1,0:T(8,128)S(1)}, f32[128,1024]{1,0:T(8,128)}, f32[128,1024]{1,0:T(8,128)S(1)}, f32[128,1024]{1,0:T(8,128)S(1)}) custom-call(s32[2]{0:T(128)S(1)} %pad_add_fusion.idx_ref, f32[128,4096]{1,0:T(8,128)S(1)} %copy-done, f32[33,4096]{1,0:T(8,128)S(1)} %copy-done.1), custom_call_target="tpu_custom_call" | custom-call | tf_op jit(solution)/shard_map/smear/pallas_call | solution.py:119
  14.1 1.5 collective-permute-start
  15.6 2.7 %collective-permute-start.1 = (f32[128,1024]{1,0:T(8,128)S(1)}, f32[128,1024]{1,0:T(8,128)S(1)}, u32[]{:S(2)}, u32[]{:S(2)}) collective-permute-start(f32[128,1024]{1,0:T(8,128)S(1)} %get-tuple-element.26), channel_id=1, source_target_pairs={{0,8},{4,12},{8,0},{12,4},{1,9},{5,13},{9,1},{13,5},{2,10},{6,14},... | collective-permute-start | bytes 1572872 | tf_op jit(solution)/shard_map/ppermute | solution.py:193
  19.8 4.5 %all-to-all-start = ((f32[4,256,128]{2,1,0:T(8,128)}), f32[4,256,128]{2,1,0:T(8,128)}, u32[]{:S(2)}, u32[]{:S(2)}) async-start(f32[4,256,128]{2,1,0:T(8,128)} %broadcast_in_dim.16), calls=%async_computation | async-start | bytes 1048576 | tf_op jit(solution)/shard_map/all_to_all | solution.py:198
  25.2 7.8 %all-to-all-done = f32[4,256,128]{2,1,0:T(8,128)} async-done(((f32[4,256,128]{2,1,0:T(8,128)}), f32[4,256,128]{2,1,0:T(8,128)}, u32[]{:S(2)}, u32[]{:S(2)}) %all-to-all-start) | async-done | bytes 524320 | tf_op jit(solution)/shard_map/all_to_all | solution.py:198
  34.1 7.5 %collective-permute-done.1.x2 = f32[128,1024]{1,0:T(8,128)S(1)} collective-permute-done((f32[128,1024]{1,0:T(8,128)S(1)}, f32[128,1024]{1,0:T(8,128)S(1)}, u32[]{:S(2)}, u32[]{:S(2)}) %collective-permute-start.1) | collective-permute-done | bytes 524320 | tf_op jit(solution)/shard_map/ppermute | solution.py:193
  41.5 2.4 collective-permute-done.2.x3
  43.9 3.0 %components_part.3 = (f32[520,128]{1,0:T(8,128)S(1)}, f32[520,128]{1,0:T(8,128)S(1)}) custom-call(f32[128,1024]{1,0:T(8,128)S(1)} %get-tuple-element.24.x0, f32[128,1024]{1,0:T(8,128)S(1)} %collective-permute-done.x1, f32[128,1024]{1,0:T(8,128)S(1)} %collective-permute-done.1.x2, f32[128,1024]{1,0:T(8,128)S(1)} %collective-permute-done.2.x3, ...), custom_call_target="tpu_custom_call" | custom-call | tf_op jit(solution)/shard_map/components_part/pallas_call | solution.py:155
  47.0 1.5 collective-permute-done.3
  49.4 11.4 %all-to-all-start.1 = ((f32[32,24,128]{2,1,0:T(8,128)}), f32[32,24,128]{2,1,0:T(8,128)S(1)}, u32[]{:S(2)}, u32[]{:S(2)}) async-start(f32[32,24,128]{2,1,0:T(8,128)} %pad_maximum_fusion), calls=%async_computation.1 | async-start | bytes 786432 | tf_op jit(solution)/shard_map/all_to_all | solution.py:223
  60.8 15.0 %all-to-all-done.1 = f32[32,24,128]{2,1,0:T(8,128)S(1)} async-done(((f32[32,24,128]{2,1,0:T(8,128)}), f32[32,24,128]{2,1,0:T(8,128)S(1)}, u32[]{:S(2)}, u32[]{:S(2)}) %all-to-all-start.1) | async-done | bytes 393248 | tf_op jit(solution)/shard_map/all_to_all | solution.py:223
  76.6 16.1 %all_to_all.40 = f32[32,16,128]{2,1,0:T(8,128)S(1)} all-to-all(f32[32,16,128]{2,1,0:T(8,128)S(1)} %broadcast_in_dim.18), channel_id=1, replica_groups=mesh['z'=8,'c'=2,'x'=4,'y'=4] {'z','y'}, dimensions={0} | all-to-all | bytes 524288 | tf_op jit(solution)/shard_map/all_to_all | solution.py:198
  92.7 1.5 collective-permute-done.4.hb
  94.2 2.2 loadings_part.3
  96.5 1.9 collective-permute-start.6
  98.4 2.8 %collective-permute-start.7 = (f32[136,128]{1,0:T(8,128)S(1)}, f32[136,128]{1,0:T(8,128)S(1)}, u32[]{:S(2)}, u32[]{:S(2)}) collective-permute-start(f32[136,128]{1,0:T(8,128)S(1)} %get-tuple-element.33), channel_id=1, source_target_pairs={{0,12},{4,8},{8,4},{12,0},{1,13},{5,9},{9,5},{13,1},{2,14},{6,10},... | collective-permute-start | bytes 208904 | tf_op jit(solution)/shard_map/ppermute | solution.py:193
  102.4 1.5 collective-permute-done.7
  104.0 2.8 %collective-permute-start.10 = (f32[128,128]{1,0:T(8,128)S(1)}, f32[128,128]{1,0:T(8,128)S(1)}, u32[]{:S(2)}, u32[]{:S(2)}) collective-permute-start(f32[128,128]{1,0:T(8,128)S(1)} %fusion.2.l0), channel_id=1, source_target_pairs={{0,12},{4,8},{8,4},{12,0},{1,13},{5,9},{9,5},{13,1},{2,14},{6,10},... | collective-permute-start | bytes 196616 | tf_op jit(solution)/shard_map/ppermute | solution.py:193
  106.8 1.3 collective-permute-start.8
  108.2 2.1 collective-permute-done.10.l3
  110.3 2.3 collective-permute-done.9.l2
  112.6 3.1 %components_part.4 = (f32[520,128]{1,0:T(8,128)S(1)}, f32[520,128]{1,0:T(8,128)S(1)}) custom-call(f32[128,1024]{1,0:T(8,128)S(1)} %get-tuple-element.24.x0, f32[128,1024]{1,0:T(8,128)S(1)} %collective-permute-done.x1, f32[128,1024]{1,0:T(8,128)S(1)} %collective-permute-done.1.x2, f32[128,1024]{1,0:T(8,128)S(1)} %collective-permute-done.2.x3, ...), custom_call_target="tpu_custom_call" | custom-call | tf_op jit(solution)/shard_map/components_part/pallas_call | solution.py:155
  115.8 1.5 collective-permute-done.11
  117.4 19.5 %all_to_all.41 = f32[32,24,128]{2,1,0:T(8,128)S(1)} all-to-all(f32[32,24,128]{2,1,0:T(8,128)S(1)} %pad_maximum_fusion.1), channel_id=1, replica_groups=mesh['z'=8,'c'=2,'x'=4,'y'=4] {'z','y'}, dimensions={0} | all-to-all | bytes 786432 | tf_op jit(solution)/shard_map/all_to_all | solution.py:223
  137.0 16.1 %all_to_all.42 = f32[32,16,128]{2,1,0:T(8,128)S(1)} all-to-all(f32[32,16,128]{2,1,0:T(8,128)S(1)} %broadcast_in_dim.20), channel_id=1, replica_groups=mesh['z'=8,'c'=2,'x'=4,'y'=4] {'z','y'}, dimensions={0} | all-to-all | bytes 524288 | tf_op jit(solution)/shard_map/all_to_all | solution.py:198
  153.1 1.5 collective-permute-done.12.hb
  154.6 2.2 loadings_part.4
  156.9 2.7 %collective-permute-start.14 = (f32[136,128]{1,0:T(8,128)S(1)}, f32[136,128]{1,0:T(8,128)S(1)}, u32[]{:S(2)}, u32[]{:S(2)}) collective-permute-start(f32[136,128]{1,0:T(8,128)S(1)} %get-tuple-element.38), channel_id=1, source_target_pairs={{0,8},{4,12},{8,0},{12,4},{1,9},{5,13},{9,1},{13,5},{2,10},{6,14},... | collective-permute-start | bytes 208904 | tf_op jit(solution)/shard_map/ppermute | solution.py:193
  159.6 2.0 collective-permute-start.15
  161.6 1.8 collective-permute-done.14
  163.4 1.7 collective-permute-done.15
  165.2 2.1 collective-permute-start.18
  167.7 1.7 collective-permute-start.16
  169.3 1.9 collective-permute-done.18.l3
  171.3 1.7 collective-permute-done.17.l2
  173.0 3.0 %components_part.5 = (f32[520,128]{1,0:T(8,128)S(1)}, f32[520,128]{1,0:T(8,128)S(1)}) custom-call(f32[128,1024]{1,0:T(8,128)S(1)} %get-tuple-element.24.x0, f32[128,1024]{1,0:T(8,128)S(1)} %collective-permute-done.x1, f32[128,1024]{1,0:T(8,128)S(1)} %collective-permute-done.1.x2, f32[128,1024]{1,0:T(8,128)S(1)} %collective-permute-done.2.x3, ...), custom_call_target="tpu_custom_call" | custom-call | tf_op jit(solution)/shard_map/components_part/pallas_call | solution.py:155
  176.4 1.5 collective-permute-done.19
  178.0 19.5 %all_to_all.43 = f32[32,24,128]{2,1,0:T(8,128)S(1)} all-to-all(f32[32,24,128]{2,1,0:T(8,128)S(1)} %pad_maximum_fusion.2), channel_id=1, replica_groups=mesh['z'=8,'c'=2,'x'=4,'y'=4] {'z','y'}, dimensions={0} | all-to-all | bytes 786432 | tf_op jit(solution)/shard_map/all_to_all | solution.py:223
  197.6 16.1 %all_to_all.44 = f32[32,16,128]{2,1,0:T(8,128)S(1)} all-to-all(f32[32,16,128]{2,1,0:T(8,128)S(1)} %broadcast_in_dim.22), channel_id=1, replica_groups=mesh['z'=8,'c'=2,'x'=4,'y'=4] {'z','y'}, dimensions={0} | all-to-all | bytes 524288 | tf_op jit(solution)/shard_map/all_to_all | solution.py:198
  213.7 1.5 collective-permute-done.20.hb
  215.2 2.2 loadings_part.5
  218.1 2.1 collective-permute-start.22
  220.2 2.0 collective-permute-start.23
  222.2 1.8 collective-permute-done.22
  224.0 1.7 collective-permute-done.23
  226.8 4.1 %all-to-all-start.7 = ((f32[16,128,128]{2,1,0:T(8,128)}), f32[16,128,128]{2,1,0:T(8,128)S(1)}, u32[]{:S(2)}, u32[]{:S(2)}) async-start(f32[16,128,128]{2,1,0:T(8,128)} %broadcast_in_dim.23), calls=%async_computation.7 | async-start | bytes 2097152 | tf_op jit(solution)/shard_map/all_to_all | solution.py:198
  231.8 15.3 %all-to-all-done.7 = f32[16,128,128]{2,1,0:T(8,128)S(1)} async-done(((f32[16,128,128]{2,1,0:T(8,128)}), f32[16,128,128]{2,1,0:T(8,128)S(1)}, u32[]{:S(2)}, u32[]{:S(2)}) %all-to-all-start.7) | async-done | bytes 1048608 | tf_op jit(solution)/shard_map/all_to_all | solution.py:198
  (69 shorter events, 12.8 us)
Async XLA Ops:
  0.7 1.6 copy-start
  2.3 1.1 copy-start.1
  3.4 15.4 %copy-start.2 = (f32[128,256]{1,0:T(8,128)S(1)}, f32[128,256]{1,0:T(8,128)}, u32[]{:S(2)}) copy-start(f32[128,256]{1,0:T(8,128)} %param.7) | copy-start | bytes 393220
  14.1 19.9 %collective-permute-start = (f32[128,1024]{1,0:T(8,128)}, f32[128,1024]{1,0:T(8,128)S(1)}, u32[]{:S(2)}, u32[]{:S(2)}) collective-permute-start(f32[128,1024]{1,0:T(8,128)} %get-tuple-element.25), channel_id=1, source_target_pairs={{0,4},{4,0},{8,12},{12,8},{1,5},{5,1},{9,13},{13,9},{2,6},{6,2},{1... | collective-permute-start | bytes 1572872 | tf_op jit(solution)/shard_map/ppermute | solution.py:193
  15.6 25.9 %collective-permute-start.1 = (f32[128,1024]{1,0:T(8,128)S(1)}, f32[128,1024]{1,0:T(8,128)S(1)}, u32[]{:S(2)}, u32[]{:S(2)}) collective-permute-start(f32[128,1024]{1,0:T(8,128)S(1)} %get-tuple-element.26), channel_id=1, source_target_pairs={{0,8},{4,12},{8,0},{12,4},{1,9},{5,13},{9,1},{13,5},{2,10},{6,14},... | collective-permute-start | bytes 1572872 | tf_op jit(solution)/shard_map/ppermute | solution.py:193
  18.4 25.5 %collective-permute-start.2 = (f32[128,1024]{1,0:T(8,128)S(1)}, f32[128,1024]{1,0:T(8,128)S(1)}, u32[]{:S(2)}, u32[]{:S(2)}) collective-permute-start(f32[128,1024]{1,0:T(8,128)S(1)} %get-tuple-element.27), channel_id=1, source_target_pairs={{0,12},{4,8},{8,4},{12,0},{1,13},{5,9},{9,5},{13,1},{2,14},{6,10},... | collective-permute-start | bytes 1572872 | tf_op jit(solution)/shard_map/ppermute | solution.py:193
  19.8 13.2 %all-to-all-start = ((f32[4,256,128]{2,1,0:T(8,128)}), f32[4,256,128]{2,1,0:T(8,128)}, u32[]{:S(2)}, u32[]{:S(2)}) async-start(f32[4,256,128]{2,1,0:T(8,128)} %broadcast_in_dim.16), calls=%async_computation | async-start | bytes 1048576 | tf_op jit(solution)/shard_map/all_to_all | solution.py:198
  46.9 1.6 collective-permute-start.3
  49.4 26.4 %all-to-all-start.1 = ((f32[32,24,128]{2,1,0:T(8,128)}), f32[32,24,128]{2,1,0:T(8,128)S(1)}, u32[]{:S(2)}, u32[]{:S(2)}) async-start(f32[32,24,128]{2,1,0:T(8,128)} %pad_maximum_fusion), calls=%async_computation.1 | async-start | bytes 786432 | tf_op jit(solution)/shard_map/all_to_all | solution.py:223
  92.7 1.5 collective-permute-start.4
  96.4 5.0 %collective-permute-start.5 = (f32[136,128]{1,0:T(8,128)S(1)}, f32[136,128]{1,0:T(8,128)S(1)}, u32[]{:S(2)}, u32[]{:S(2)}) collective-permute-start(f32[136,128]{1,0:T(8,128)S(1)} %get-tuple-element.31), channel_id=1, source_target_pairs={{0,4},{4,0},{8,12},{12,8},{1,5},{5,1},{9,13},{13,9},{2,6},{6,2},{1... | collective-permute-start | bytes 208904 | tf_op jit(solution)/shard_map/ppermute | solution.py:193
  96.5 6.0 %collective-permute-start.6 = (f32[136,128]{1,0:T(8,128)S(1)}, f32[136,128]{1,0:T(8,128)S(1)}, u32[]{:S(2)}, u32[]{:S(2)}) collective-permute-start(f32[136,128]{1,0:T(8,128)S(1)} %get-tuple-element.32), channel_id=1, source_target_pairs={{0,8},{4,12},{8,0},{12,4},{1,9},{5,13},{9,1},{13,5},{2,10},{6,14},... | collective-permute-start | bytes 208904 | tf_op jit(solution)/shard_map/ppermute | solution.py:193
  98.4 5.5 %collective-permute-start.7 = (f32[136,128]{1,0:T(8,128)S(1)}, f32[136,128]{1,0:T(8,128)S(1)}, u32[]{:S(2)}, u32[]{:S(2)}) collective-permute-start(f32[136,128]{1,0:T(8,128)S(1)} %get-tuple-element.33), channel_id=1, source_target_pairs={{0,12},{4,8},{8,4},{12,0},{1,13},{5,9},{9,5},{13,1},{2,14},{6,10},... | collective-permute-start | bytes 208904 | tf_op jit(solution)/shard_map/ppermute | solution.py:193
  104.0 6.3 %collective-permute-start.10 = (f32[128,128]{1,0:T(8,128)S(1)}, f32[128,128]{1,0:T(8,128)S(1)}, u32[]{:S(2)}, u32[]{:S(2)}) collective-permute-start(f32[128,128]{1,0:T(8,128)S(1)} %fusion.2.l0), channel_id=1, source_target_pairs={{0,12},{4,8},{8,4},{12,0},{1,13},{5,9},{9,5},{13,1},{2,14},{6,10},... | collective-permute-start | bytes 196616 | tf_op jit(solution)/shard_map/ppermute | solution.py:193
  106.8 5.8 %collective-permute-start.9 = (f32[128,128]{1,0:T(8,128)S(1)}, f32[128,128]{1,0:T(8,128)S(1)}, u32[]{:S(2)}, u32[]{:S(2)}) collective-permute-start(f32[128,128]{1,0:T(8,128)S(1)} %fusion.2.l0), channel_id=1, source_target_pairs={{0,8},{4,12},{8,0},{12,4},{1,9},{5,13},{9,1},{13,5},{2,10},{6,14},... | collective-permute-start | bytes 196616 | tf_op jit(solution)/shard_map/ppermute | solution.py:193
  106.8 5.8 %collective-permute-start.8 = (f32[128,128]{1,0:T(8,128)S(1)}, f32[128,128]{1,0:T(8,128)S(1)}, u32[]{:S(2)}, u32[]{:S(2)}) collective-permute-start(f32[128,128]{1,0:T(8,128)S(1)} %fusion.2.l0), channel_id=1, source_target_pairs={{0,4},{4,0},{8,12},{12,8},{1,5},{5,1},{9,13},{13,9},{2,6},{6,2},{1... | collective-permute-start | bytes 196616 | tf_op jit(solution)/shard_map/ppermute | solution.py:193
  115.7 1.6 collective-permute-start.11
  153.1 1.5 collective-permute-start.12
  156.8 4.8 %collective-permute-start.13 = (f32[136,128]{1,0:T(8,128)S(1)}, f32[136,128]{1,0:T(8,128)S(1)}, u32[]{:S(2)}, u32[]{:S(2)}) collective-permute-start(f32[136,128]{1,0:T(8,128)S(1)} %get-tuple-element.37), channel_id=1, source_target_pairs={{0,4},{4,0},{8,12},{12,8},{1,5},{5,1},{9,13},{13,9},{2,6},{6,2},{1... | collective-permute-start | bytes 208904 | tf_op jit(solution)/shard_map/ppermute | solution.py:193
  156.9 6.5 %collective-permute-start.14 = (f32[136,128]{1,0:T(8,128)S(1)}, f32[136,128]{1,0:T(8,128)S(1)}, u32[]{:S(2)}, u32[]{:S(2)}) collective-permute-start(f32[136,128]{1,0:T(8,128)S(1)} %get-tuple-element.38), channel_id=1, source_target_pairs={{0,8},{4,12},{8,0},{12,4},{1,9},{5,13},{9,1},{13,5},{2,10},{6,14},... | collective-permute-start | bytes 208904 | tf_op jit(solution)/shard_map/ppermute | solution.py:193
  159.6 5.5 %collective-permute-start.15 = (f32[136,128]{1,0:T(8,128)S(1)}, f32[136,128]{1,0:T(8,128)S(1)}, u32[]{:S(2)}, u32[]{:S(2)}) collective-permute-start(f32[136,128]{1,0:T(8,128)S(1)} %get-tuple-element.39), channel_id=1, source_target_pairs={{0,12},{4,8},{8,4},{12,0},{1,13},{5,9},{9,5},{13,1},{2,14},{6,10},... | collective-permute-start | bytes 208904 | tf_op jit(solution)/shard_map/ppermute | solution.py:193
  165.2 6.1 %collective-permute-start.18 = (f32[128,128]{1,0:T(8,128)S(1)}, f32[128,128]{1,0:T(8,128)S(1)}, u32[]{:S(2)}, u32[]{:S(2)}) collective-permute-start(f32[128,128]{1,0:T(8,128)S(1)} %fusion.1.l0), channel_id=1, source_target_pairs={{0,12},{4,8},{8,4},{12,0},{1,13},{5,9},{9,5},{13,1},{2,14},{6,10},... | collective-permute-start | bytes 196616 | tf_op jit(solution)/shard_map/ppermute | solution.py:193
  167.2 5.8 %collective-permute-start.17 = (f32[128,128]{1,0:T(8,128)S(1)}, f32[128,128]{1,0:T(8,128)S(1)}, u32[]{:S(2)}, u32[]{:S(2)}) collective-permute-start(f32[128,128]{1,0:T(8,128)S(1)} %fusion.1.l0), channel_id=1, source_target_pairs={{0,8},{4,12},{8,0},{12,4},{1,9},{5,13},{9,1},{13,5},{2,10},{6,14},... | collective-permute-start | bytes 196616 | tf_op jit(solution)/shard_map/ppermute | solution.py:193
  167.7 5.3 %collective-permute-start.16 = (f32[128,128]{1,0:T(8,128)S(1)}, f32[128,128]{1,0:T(8,128)S(1)}, u32[]{:S(2)}, u32[]{:S(2)}) collective-permute-start(f32[128,128]{1,0:T(8,128)S(1)} %fusion.1.l0), channel_id=1, source_target_pairs={{0,4},{4,0},{8,12},{12,8},{1,5},{5,1},{9,13},{13,9},{2,6},{6,2},{1... | collective-permute-start | bytes 196616 | tf_op jit(solution)/shard_map/ppermute | solution.py:193
  176.1 1.8 collective-permute-start.19
  213.7 1.5 collective-permute-start.20
  217.4 4.8 %collective-permute-start.21 = (f32[136,128]{1,0:T(8,128)S(1)}, f32[136,128]{1,0:T(8,128)S(1)}, u32[]{:S(2)}, u32[]{:S(2)}) collective-permute-start(f32[136,128]{1,0:T(8,128)S(1)} %get-tuple-element.43), channel_id=1, source_target_pairs={{0,4},{4,0},{8,12},{12,8},{1,5},{5,1},{9,13},{13,9},{2,6},{6,2},{1... | collective-permute-start | bytes 208904 | tf_op jit(solution)/shard_map/ppermute | solution.py:193
  218.1 5.9 %collective-permute-start.22 = (f32[136,128]{1,0:T(8,128)S(1)}, f32[136,128]{1,0:T(8,128)S(1)}, u32[]{:S(2)}, u32[]{:S(2)}) collective-permute-start(f32[136,128]{1,0:T(8,128)S(1)} %get-tuple-element.44), channel_id=1, source_target_pairs={{0,8},{4,12},{8,0},{12,4},{1,9},{5,13},{9,1},{13,5},{2,10},{6,14},... | collective-permute-start | bytes 208904 | tf_op jit(solution)/shard_map/ppermute | solution.py:193
  220.2 5.5 %collective-permute-start.23 = (f32[136,128]{1,0:T(8,128)S(1)}, f32[136,128]{1,0:T(8,128)S(1)}, u32[]{:S(2)}, u32[]{:S(2)}) collective-permute-start(f32[136,128]{1,0:T(8,128)S(1)} %get-tuple-element.45), channel_id=1, source_target_pairs={{0,12},{4,8},{8,4},{12,0},{1,13},{5,9},{9,5},{13,1},{2,14},{6,10},... | collective-permute-start | bytes 208904 | tf_op jit(solution)/shard_map/ppermute | solution.py:193
  226.8 20.2 %all-to-all-start.7 = ((f32[16,128,128]{2,1,0:T(8,128)}), f32[16,128,128]{2,1,0:T(8,128)S(1)}, u32[]{:S(2)}, u32[]{:S(2)}) async-start(f32[16,128,128]{2,1,0:T(8,128)} %broadcast_in_dim.23), calls=%async_computation.7 | async-start | bytes 2097152 | tf_op jit(solution)/shard_map/all_to_all | solution.py:198

commit v2 on v0

v2 whole, which is shorter than its diff:
```python
import functools
import jax
import jax.numpy as jnp
from jax import lax
from jax.experimental import pallas as pl
from jax.experimental.pallas import tpu as pltpu
from jax.sharding import Mesh, PartitionSpec as P

RADIUS = 16
TAPS = 33
ITERS = 3
LANES = 128
VMEM = pltpu.MemorySpace.VMEM
SMEM = pltpu.MemorySpace.SMEM
F32 = jnp.float32
BF16 = jnp.bfloat16
NT = ((1,), (1,))
NN = ((1,), (0,))


def split(x):
    hi = x.astype(BF16)
    return hi, (x - hi.astype(F32)).astype(BF16)


def mm(a, b, dims):
    return lax.dot_general(a, b, (dims, ((), ())), preferred_element_type=F32)


def mm3(a, b, dims):
    (ah, al), (bh, bl) = a, b
    return mm(ah, bh, dims) + (mm(al, bh, dims) + mm(ah, bl, dims))


def mm_short(a, b, dims):
    (ah, al), (bh, bl) = a, b
    axis = dims[1][0]
    wide = mm(jnp.concatenate([ah, al], axis=1), jnp.concatenate([bh, bh], axis=axis), dims)
    return wide + mm(ah, bl, dims)


def block(j):
    return pl.ds(pl.multiple_of(j * LANES, LANES), LANES)


def call(kernel, outs, ins, name, macs, scratch=(), scalars=0, aliases=None):
    cost = 1024 if name == "smear" else 1 << 20
    kept = [jax.ShapeDtypeStruct(ins[i].shape, ins[i].dtype) for i in (aliases or {})]
    result = pl.pallas_call(
        kernel,
        out_shape=[jax.ShapeDtypeStruct(o, F32) for o in outs] + kept,
        in_specs=[pl.BlockSpec(memory_space=SMEM)] * scalars + [pl.BlockSpec(memory_space=VMEM)] * (len(ins) - scalars),
        out_specs=[pl.BlockSpec(memory_space=VMEM)] * (len(outs) + len(kept)),
        scratch_shapes=list(scratch),
        input_output_aliases=aliases or {},
        compiler_params=pltpu.CompilerParams(vmem_limit_bytes=16 << 20),
        cost_estimate=pl.CostEstimate(flops=cost, bytes_accessed=cost, transcendentals=0),
        name=name,
    )(*ins)
    return result


def bands_kernel(blocks, res_ref, bh, bl, pad):
    zero = jnp.zeros((LANES, 2 * LANES), BF16)
    for ref in (bh, bl):
        ref[0:LANES, :] = zero
        ref[(blocks + 1) * LANES : (blocks + 2) * LANES, :] = zero
    for ref in pad:
        ref[...] = jnp.zeros((LANES, LANES), F32)
    row = lax.broadcasted_iota(jnp.int32, (LANES, LANES), 0)
    col = lax.broadcasted_iota(jnp.int32, (LANES, LANES), 1)
    inside = jnp.abs(row - col) <= RADIUS

    def one(j, ref):
        ref[0:TAPS, :] = res_ref[:, block(j)]
        band = pltpu.roll(jnp.transpose(ref[...]), LANES - RADIUS, 1, stride=1, stride_axis=0)
        h, l = split(jnp.where(inside, band, 0.0))
        bh[block(j + 1), 0:LANES] = h
        bl[block(j + 1), 0:LANES] = l
        h, l = split(jnp.where(inside, 0.0, band))
        bh[block(j + 1), LANES:] = h
        bl[block(j + 1), LANES:] = l

    def step(i, carry):
        for u, ref in enumerate(pad):
            one(i * len(pad) + u, ref)
        return carry

    lax.fori_loop(0, blocks // len(pad), step, 0)


def make_bands(resolution):
    blocks = resolution.shape[1] // LANES
    shape = jax.ShapeDtypeStruct(((blocks + 2) * LANES, 2 * LANES), BF16)

    def kernel(res_ref, bh, bl, p0, p1, p2, p3):
        bands_kernel(blocks, res_ref, bh, bl, (p0, p1, p2, p3))

    return pl.pallas_call(
        kernel,
        out_shape=[shape] * 2,
        in_specs=[pl.BlockSpec(memory_space=VMEM)],
        out_specs=[pl.BlockSpec(memory_space=VMEM)] * 2,
        scratch_shapes=[pltpu.VMEM((LANES, LANES), F32)] * 4,
        compiler_params=pltpu.CompilerParams(vmem_limit_bytes=16 << 20),
        cost_estimate=pl.CostEstimate(flops=1 << 20, bytes_accessed=12 << 20, transcendentals=0),
        name="bands",
    )(resolution)


def smear_kernel(blocks, d, idx_ref, field_ref, bh_ref, bl_ref, out, token, _, __, ___, vh, vl, uh, ul):
    token[...] = jnp.zeros(token.shape, F32)
    rows = field_ref.shape[0]
    per = blocks // 4
    base = (idx_ref[0] ^ d) * per
    flip = idx_ref[1] * (per // 2)
    near = lax.broadcasted_iota(jnp.int32, (rows, LANES), 1) < LANES // 2

    def field(j):
        return field_ref[:, block(jnp.clip(j, 0, blocks - 1))]

    def at(i):
        return slice(i * LANES, (i + 1) * LANES)

    def window(ref, i):
        return jnp.concatenate([ref[:, at(i)], jnp.where(near, ref[:, at(i + 1)], ref[:, at(i - 1)])], axis=1)

    for i in range(per + 4):
        v = field(base + i - 2)
        if i < 2:
            v = jnp.where(base > 0, v, 0.0)
        if i >= per + 2:
            v = jnp.where(base + per < blocks, v, 0.0)
        vh[:, at(i)], vl[:, at(i)] = split(v)
    for i in range(per + 2):
        band = block(base + i)
        blurred = mm3((window(vh, i + 1), window(vl, i + 1)), (bh_ref[band, :], bl_ref[band, :]), NT)
        u = field(base + i - 1) / blurred
        if i < 1:
            u = jnp.where(base > 0, u, 0.0)
        if i >= per + 1:
            u = jnp.where(base + per < blocks, u, 0.0)
        uh[:, at(i)], ul[:, at(i)] = split(u)

    def stack(ref, j):
        half = LANES // 2
        after = ref[pl.ds(pl.multiple_of((j + 1) * LANES, LANES), half), LANES:]
        before = ref[pl.ds(pl.multiple_of((j - 1) * LANES + half, half), half), LANES:]
        return jnp.concatenate([ref[block(j), 0:LANES], after, before], axis=0)

    for i in range(per):
        bh = stack(bh_ref, base + i + 1)
        bl = stack(bl_ref, base + i + 1)
        total = mm3((window(uh, i + 1), window(ul, i + 1)), (bh, bl), NN)
        weight = jnp.sum(bh.astype(F32) + bl.astype(F32), axis=0, keepdims=True)
        out[:, block(i ^ flip)] = field(base + i) * total / weight


def smear(d, idx, field, bh, bl):
    rows, width = field.shape
    blocks = width // LANES
    per = blocks // 4
    scratch = [pltpu.VMEM((rows, (per + 4) * LANES), BF16)] * 2 + [pltpu.VMEM((rows, (per + 2) * LANES), BF16)] * 2
    return call(
        functools.partial(smear_kernel, blocks, d),
        [(rows, width // 4), (8, LANES)],
        [idx, field, bh, bl],
        "smear",
        rows * width * LANES,
        scratch,
        1,
        {1: 2, 2: 3, 3: 4},
    )


def fold(x):
    return jnp.sum(jnp.sum(x.reshape(4, x.shape[0] // 32, 8, x.shape[1]), axis=1), axis=0)


def numerator(x, loads, pair, tile):
    return mm_short(split(jnp.transpose(loads)), split(x / mm_short(split(loads), pair, NT)), NN)


def first_kernel(l, h, x, out, sums):
    half = h.shape[0]
    out[...] = numerator(x[:, half:], l[...], split(h[...]), half)
    sums[...] = fold(l[...])


def middle_kernel(l, h, x, before, before_sums, out, sums):
    half = h.shape[0]
    out[...] = before[...] + numerator(x[:, half:], l[...], split(h[...]), half)
    sums[...] = before_sums[...] + fold(l[...])


def last_kernel(l, h, x, before, before_sums, out):
    half = h.shape[0]
    out[0:half, :] = jnp.transpose(before[...] + numerator(x[:, half:], l[...], split(h[...]), half))
    out[half : half + 8, :] = before_sums[...] + fold(l[...])


def keep_kernel(x0, x1, x2, x3, l0, l1, l2, l3, h_ref, out):
    half = h_ref.shape[0]
    loads = jnp.concatenate([l[...] for l in (l0, l1, l2, l3)], axis=0)
    left, left_t = split(loads), split(jnp.transpose(loads))
    tile = 256
    for t in range(half // tile):
        h = split(h_ref[t * tile : (t + 1) * tile, :])
        x = jnp.concatenate([r[:, t * tile : (t + 1) * tile] for r in (x0, x1, x2, x3)], axis=0)
        quotient = split(x / mm_short(left, h, NT))
        out[t * tile : (t + 1) * tile, :] = jnp.transpose(mm3(left_t, quotient, NN))
    out[half : half + 8, :] = fold(loads)


def components_part(xs, ls, mine, theirs, order):
    half, comps = mine.shape
    rows = xs[0].shape[0]
    macs = 2 * rows * half * comps
    a, b, c, d = order
    state = call(first_kernel, [(comps, half), (8, comps)], [ls[a], theirs, xs[a]], "components_first", macs)
    state = call(middle_kernel, [(comps, half), (8, comps)], [ls[b], theirs, xs[b], *state], "components_middle", macs)
    state = call(middle_kernel, [(comps, half), (8, comps)], [ls[c], theirs, xs[c], *state], "components_middle", macs)
    send = call(last_kernel, [(half + 8, comps)], [ls[d], theirs, xs[d], *state], "components_last", macs)[0]
    keep = call(keep_kernel, [(half + 8, comps)], [*xs, *ls, mine], "components_keep", 4 * macs)[0]
    return keep, send


def own_half_kernel(x0, x1, x2, x3, l0, l1, l2, l3, h_ref, o0, o1, o2, o3):
    pair = split(h_ref[...])
    half = h_ref.shape[0]
    for x, l, out in zip((x0, x1, x2, x3), (l0, l1, l2, l3), (o0, o1, o2, o3)):
        out[...] = mm3(split(x[:, 0:half] / mm_short(split(l[...]), pair, NT)), pair, NN)


def other_half_kernel(x, l, h_ref, own, before, out):
    pair = split(h_ref[...])
    half = h_ref.shape[0]
    rows = l.shape[0]
    out[0:rows, :] = before[...] + mm3(split(x[:, half:] / mm_short(split(l[...]), pair, NT)), pair, NN)
    out[rows : rows + 8, :] = fold(h_ref[...]) + fold(own[...])


def loadings_part(xs, ls, mine, theirs):
    half, comps = mine.shape
    rows = xs[0].shape[0]
    macs = 2 * rows * half * comps
    first = call(own_half_kernel, [(rows, comps)] * 4, [*xs, *ls, mine], "loadings_own", 4 * macs)
    return [
        call(other_half_kernel, [(rows + 8, comps)], [xs[d], ls[d], theirs, mine, first[d]], "loadings_other", macs)[0]
        for d in range(4)
    ]


SPLIT = ("z", "c", "x", "y")


def swap(x, axis, distance):
    size = 2 if axis == "c" else 4
    return lax.ppermute(x, axis, [(i, i ^ distance) for i in range(size)])


def spread(x, axes, copies):
    y = jnp.broadcast_to(x[None], (copies,) + x.shape)
    return lax.all_to_all(y, axes, 0, 0).reshape((-1,) + x.shape[1:])


def local(measured, resolution, loadings_start, components_start):
    xi, yi, ci = lax.axis_index("x"), lax.axis_index("y"), lax.axis_index("c")
    zi = lax.axis_index("z")
    comps = components_start.shape[0]
    idx = jnp.stack([xi, ci]).astype(jnp.int32)
    bh, bl = make_bands(resolution)
    field = measured
    xs = [None] * 4
    for d in (2, 1, 3, 0):
        xs[d], zero, field, bh, bl = smear(d, idx, field, bh, bl)
        if d:
            xs[d] = swap(xs[d], "x", d)
    start = spread((components_start + zero[0, 0]).T, "y", 4)
    half = start.shape[0] // 2
    mine = lax.dynamic_slice_in_dim(start, ci * half, half)
    theirs = lax.dynamic_slice_in_dim(start, (1 - ci) * half, half)
    rows = measured.shape[0]
    ls = [lax.dynamic_slice_in_dim(loadings_start, ((xi ^ d) * 4 + yi) * rows, rows) for d in range(4)]
    group = 32
    part = half // group
    piece = lax.dynamic_slice_in_dim(mine, (zi * 4 + yi) * part, part)
    for step in range(ITERS):
        keep, send = components_part(xs, ls, mine, theirs, (0, 1, 3, 2) if step else (0, 2, 1, 3))
        both = keep + swap(send, "c", 1)
        totals = jnp.sum(both[half:], axis=0)
        packed = jnp.concatenate(
            [both[:half].reshape(group, part, 1, comps), jnp.broadcast_to(totals, (group, 1, 1, comps))], axis=1
        )
        total = jnp.sum(lax.all_to_all(packed, ("z", "y"), 0, 0), axis=0)[:, 0]
        piece = piece * total[:part] / total[part:]
        mine = spread(piece, ("z", "y"), group)
        theirs = swap(mine, "c", 1)
        parts = loadings_part(xs, ls, mine, theirs)
        total = parts[0] + swap(parts[2], "x", 2) + swap(parts[1], "x", 1) + swap(parts[3], "x", 3)
        own = ls[0] * total[:rows] / jnp.sum(total[rows:], axis=0, keepdims=True)
        if step < ITERS - 1:
            ls = [own] + [swap(own, "x", d) for d in (1, 2, 3)]
    loadings = spread(own, ("x", "y"), 16)
    low = lax.dynamic_slice_in_dim(mine, (yi % 2) * (half // 2), half // 2)
    high = lax.dynamic_slice_in_dim(theirs, (yi % 2) * (half // 2), half // 2)
    components = jnp.where(yi // 2 == ci, low, high).T
    return (loadings, components)


def solution(mesh):
    inner = Mesh(mesh.devices.reshape(8, 2, 4, 4), SPLIT)
    return jax.shard_map(
        local,
        mesh=inner,
        in_specs=(P(SPLIT, None), P(), P(("z", "c"), None), P(None, ("x", "y"))),
        out_specs=(P(("z", "c"), None), P(None, ("x", "y"))),
        check_vma=False,
    )
```

time: 801 us -> 226 us (0.28)
  waiting for transfers between devices: 421 us -> 52.4 us
  blocking collectives: 224 us -> 82.8 us
  other arithmetic: 78.2 us -> 3.04 us
  starting transfers between devices: 0.25 us -> 43.5 us
  matrix products: 43.2 us -> 0 us
  Pallas kernels: 0 us -> 32.3 us
  between operations: 14.7 us -> 1.17 us
    psum x6 -> x0, waiting for transfers between devices: 421 us -> none  [the longest x3 243 us: local(): numerator, w_totals = lax.psum((numerator, w_totals), 'pat')]
    psum x6 -> x0, blocking collectives: 189 us -> none  [the longest x3 122 us: local(): w_numer, h_totals = lax.psum((w_numer, jnp.sum(components, axis=1)), 'pb')]
    mul x3 -> x0, other arithmetic: 47.6 us -> none  [smear_back(): resolution[offset][None, :] * field]
    all_to_all x1 -> x5, blocking collectives: 35.6 us -> 82.8 us  [the longest x3 48 us: spread(): return lax.all_to_all(y, axes, 0, 0).reshape((-1,) + x.shape[1:])]
    dot_general x12 -> x0, matrix products: 43.2 us -> none  [the longest x6 20.7 us: local(): quotient = corrected / jnp.dot(loadings, components, precision=high)]
    all_to_all x0 -> x3, waiting for transfers between devices: none -> 36.4 us  [the longest x2 23.5 us: spread(): return lax.all_to_all(y, axes, 0, 0).reshape((-1,) + x.shape[1:])]
    pallas_call x0 -> x35, Pallas kernels: none -> 32.3 us  [the longest x34 30 us: call(): pl.pallas_call(kernel, out_shape=[jax.ShapeDtypeStruct(o, F32) for o in o...]
    ppermute x0 -> x24, starting transfers between devices: none -> 26.1 us  [swap(): return lax.ppermute(x, axis, [(i, i ^ distance) for i in range(size)])]
  transfers between devices with their start and end apart: 6 -> 27, of which waited for: 6 -> 22; matrix products, arithmetic and copies ran while one was open for 1% -> 2% of each run, Pallas kernels for 0% -> 11%
where the time goes in v2:
time: 226 us; the launch traced here: 225 us
  blocking collectives  82.8 us (37%)
  waiting for transfers between devices  52.4 us (23%)
  starting transfers between devices  43.5 us (19%)
  Pallas kernels  32.3 us (14%)
  local copies, waits for them, and re-layouts  10 us (4%)
  other arithmetic  3.04 us (1%)
    all_to_all x3, blocking collectives, spread(): return lax.all_to_all(y, axes, 0, 0).reshape((-1,) + x.shape[1:])  48 us
    all_to_all x2, blocking collectives, local(): total = jnp.sum(lax.all_to_all(packed, ('z', 'y'), 0, 0), axis=0)[:, 0]  34.8 us
    pallas_call x34, Pallas kernels, call(): pl.pallas_call(kernel, out_shape=[jax.ShapeDtypeStruct(o, F32) for o in o...  30 us
    ppermute x24, starting transfers between devices, swap(): return lax.ppermute(x, axis, [(i, i ^ distance) for i in range(size)])  26.1 us
    all_to_all x2, waiting for transfers between devices, spread(): return lax.all_to_all(y, axes, 0, 0).reshape((-1,) + x.shape[1:])  23.5 us
    ppermute x24, waiting for transfers between devices, swap(): return lax.ppermute(x, axis, [(i, i ^ distance) for i in range(size)])  16 us
    all_to_all x1, waiting for transfers between devices, local(): total = jnp.sum(lax.all_to_all(packed, ('z', 'y'), 0, 0), axis=0)[:, 0]  12.9 us
    all_to_all x1, starting transfers between devices, local(): total = jnp.sum(lax.all_to_all(packed, ('z', 'y'), 0, 0), axis=0)[:, 0]  9.33 us
  transfers between devices with their start and end apart: 27, of which 22 were waited for; matrix products, arithmetic and copies ran while one was open for 2% of the time, Pallas kernels for 11%

profile of v2, /device:TPU:32, one launch (start us, length us, event | category | flops | bytes accessed | tf_op | source)
XLA Modules:
  0.0 225.3 jit_solution(17589731910902873164)
XLA Ops:
  0.6 1.7 copy.39.field_ref
  2.3 2.3 %bands.1 = (bf16[4352,256]{1,0:T(8,128)(2,1)S(1)}, bf16[4352,256]{1,0:T(8,128)(2,1)S(1)}) custom-call(f32[33,4096]{1,0:T(8,128)S(1)} %copy-done.2), custom_call_target="tpu_custom_call" | custom-call | flops 1048576 | bytes 12582912 | tf_op jit(solution)/shard_map/bands/pallas_call | solution.py:99
  4.8 2.5 %smear.4 = (f32[128,1024]{1,0:T(8,128)}, f32[8,128]{1,0:T(8,128)}, f32[128,4096]{1,0:T(8,128)S(1)}, bf16[4352,256]{1,0:T(8,128)(2,1)S(1)}, bf16[4352,256]{1,0:T(8,128)(2,1)S(1)}) custom-call(s32[2]{0:T(128)S(1)} %pad_add_fusion.idx_ref, f32[128,4096]{1,0:T(8,128)S(1)} %copy.39.field_ref, ...), custom_call_target="tpu_custom_call", output_to_operand_aliasing={{2}: (1, {}), {3}: (2, {}), {4}: (3, {})} | custom-call | flops 1024 | bytes 1024 | tf_op jit(solution)/shard_map/smear/pallas_call | solution.py:49
  7.3 3.0 %collective-permute-start.1 = (f32[128,1024]{1,0:T(8,128)}, f32[128,1024]{1,0:T(8,128)S(1)}, u32[]{:S(2)}, u32[]{:S(2)}) collective-permute-start(f32[128,1024]{1,0:T(8,128)} %get-tuple-element.62), channel_id=1, source_target_pairs={{0,8},{4,12},{8,0},{12,4},{1,9},{5,13},{9,1},{13,5},{2,10},{6,14},... | collective-permute-start | bytes 1572872 | tf_op jit(solution)/shard_map/ppermute | solution.py:259
  10.3 2.5 %smear.5 = (f32[128,1024]{1,0:T(8,128)}, f32[8,128]{1,0:T(8,128)}, f32[128,4096]{1,0:T(8,128)S(1)}, bf16[4352,256]{1,0:T(8,128)(2,1)S(1)}, bf16[4352,256]{1,0:T(8,128)(2,1)S(1)}) custom-call(s32[2]{0:T(128)S(1)} %pad_add_fusion.idx_ref, f32[128,4096]{1,0:T(8,128)S(1)} %get-tuple-element.50.field_ref, ...), custom_call_target="tpu_custom_call", output_to_operand_aliasing={{2}: (1, {}), {3}: (2, {}), {4}: (3, {})} | custom-call | flops 1024 | bytes 1024 | tf_op jit(solution)/shard_map/smear/pallas_call | solution.py:49
  13.4 2.5 %smear.6 = (f32[128,1024]{1,0:T(8,128)}, f32[8,128]{1,0:T(8,128)}, f32[128,4096]{1,0:T(8,128)S(1)}, bf16[4352,256]{1,0:T(8,128)(2,1)S(1)}, bf16[4352,256]{1,0:T(8,128)(2,1)S(1)}) custom-call(s32[2]{0:T(128)S(1)} %pad_add_fusion.idx_ref, f32[128,4096]{1,0:T(8,128)S(1)} %get-tuple-element.53.field_ref, ...), custom_call_target="tpu_custom_call", output_to_operand_aliasing={{2}: (1, {}), {3}: (2, {}), {4}: (3, {})} | custom-call | flops 1024 | bytes 1024 | tf_op jit(solution)/shard_map/smear/pallas_call | solution.py:49
  15.9 1.3 copy-done
  17.8 1.6 copy-done.1
  19.4 1.7 smear.7
  22.4 0.8 broadcast_in_dim.16
  23.2 4.5 %all-to-all-start = ((f32[4,256,128]{2,1,0:T(8,128)}), f32[4,256,128]{2,1,0:T(8,128)S(1)}, u32[]{:S(2)}, u32[]{:S(2)}) async-start(f32[4,256,128]{2,1,0:T(8,128)} %broadcast_in_dim.16), calls=%async_computation | async-start | bytes 1048576 | tf_op jit(solution)/shard_map/all_to_all | solution.py:264
  27.7 1.0 constant_dynamic-slice_fusion.3
  28.7 8.0 %all-to-all-done = f32[4,256,128]{2,1,0:T(8,128)S(1)} async-done(((f32[4,256,128]{2,1,0:T(8,128)}), f32[4,256,128]{2,1,0:T(8,128)S(1)}, u32[]{:S(2)}, u32[]{:S(2)}) %all-to-all-start) | async-done | bytes 524320 | tf_op jit(solution)/shard_map/all_to_all | solution.py:264
  38.9 1.4 components_keep.3
  40.5 1.0 pad_maximum_fusion
  41.5 9.3 %all-to-all-start.1 = ((f32[32,17,1,128]{3,2,1,0:T(1,128)}), f32[32,17,1,128]{3,2,1,0:T(1,128)S(1)}, u32[]{:S(2)}, u32[]{:S(2)}) async-start(f32[32,17,1,128]{3,2,1,0:T(1,128)} %pad_maximum_fusion), calls=%async_computation.1 | async-start | bytes 557056 | tf_op jit(solution)/shard_map/all_to_all | solution.py:295
  50.8 12.9 %all-to-all-done.1 = f32[32,17,1,128]{3,2,1,0:T(1,128)S(1)} async-done(((f32[32,17,1,128]{3,2,1,0:T(1,128)}), f32[32,17,1,128]{3,2,1,0:T(1,128)S(1)}, u32[]{:S(2)}, u32[]{:S(2)}) %all-to-all-start.1) | async-done | bytes 278560 | tf_op jit(solution)/shard_map/all_to_all | solution.py:295
  64.0 16.0 %all_to_all.40 = f32[32,16,128]{2,1,0:T(8,128)S(1)} all-to-all(f32[32,16,128]{2,1,0:T(8,128)S(1)} %broadcast_in_dim.18), channel_id=1, replica_groups=mesh['z'=8,'c'=2,'x'=4,'y'=4] {'z','y'}, dimensions={0} | all-to-all | bytes 524288 | tf_op jit(solution)/shard_map/all_to_all | solution.py:264
  80.0 1.5 loadings_own.3
  82.0 2.8 %collective-permute-start.5 = (f32[136,128]{1,0:T(8,128)S(1)}, f32[136,128]{1,0:T(8,128)S(1)}, u32[]{:S(2)}, u32[]{:S(2)}) collective-permute-start(f32[136,128]{1,0:T(8,128)S(1)} %loadings_other.13), channel_id=1, source_target_pairs={{0,8},{4,12},{8,0},{12,4},{1,9},{5,13},{9,1},{13,5},{2,10},{6,14},... | collective-permute-start | bytes 208904 | tf_op jit(solution)/shard_map/ppermute | solution.py:259
  86.5 0.9 collective-permute-start.7
  88.2 1.5 collective-permute-done.6
  89.7 2.4 %collective-permute-done.7 = f32[136,128]{1,0:T(8,128)S(1)} collective-permute-done((f32[136,128]{1,0:T(8,128)S(1)}, f32[136,128]{1,0:T(8,128)S(1)}, u32[]{:S(2)}, u32[]{:S(2)}) %collective-permute-start.7) | collective-permute-done | bytes 69664 | tf_op jit(solution)/shard_map/ppermute | solution.py:259
  92.4 1.2 collective-permute-start.10
  93.6 2.7 %collective-permute-start.9 = (f32[128,128]{1,0:T(8,128)S(1)}, f32[128,128]{1,0:T(8,128)S(1)}, u32[]{:S(2)}, u32[]{:S(2)}) collective-permute-start(f32[128,128]{1,0:T(8,128)S(1)} %fusion.2.l0.l), channel_id=1, source_target_pairs={{0,8},{4,12},{8,0},{12,4},{1,9},{5,13},{9,1},{13,5},{2,10},{6,14},... | collective-permute-start | bytes 196616 | tf_op jit(solution)/shard_map/ppermute | solution.py:259
  98.5 0.9 collective-permute-done.9.l2.l
  100.1 1.4 components_keep.4
  101.9 17.4 %all_to_all.41 = f32[32,17,1,128]{3,2,1,0:T(1,128)S(1)} all-to-all(f32[32,17,1,128]{3,2,1,0:T(1,128)S(1)} %pad_maximum_fusion.1), channel_id=1, replica_groups=mesh['z'=8,'c'=2,'x'=4,'y'=4] {'z','y'}, dimensions={0} | all-to-all | bytes 557056 | tf_op jit(solution)/shard_map/all_to_all | solution.py:295
  119.6 16.0 %all_to_all.42 = f32[32,16,128]{2,1,0:T(8,128)S(1)} all-to-all(f32[32,16,128]{2,1,0:T(8,128)S(1)} %broadcast_in_dim.20), channel_id=1, replica_groups=mesh['z'=8,'c'=2,'x'=4,'y'=4] {'z','y'}, dimensions={0} | all-to-all | bytes 524288 | tf_op jit(solution)/shard_map/all_to_all | solution.py:264
  135.6 1.5 loadings_own.4
  137.6 2.8 %collective-permute-start.13 = (f32[136,128]{1,0:T(8,128)S(1)}, f32[136,128]{1,0:T(8,128)S(1)}, u32[]{:S(2)}, u32[]{:S(2)}) collective-permute-start(f32[136,128]{1,0:T(8,128)S(1)} %loadings_other.17), channel_id=1, source_target_pairs={{0,8},{4,12},{8,0},{12,4},{1,9},{5,13},{9,1},{13,5},{2,10},{6,14},... | collective-permute-start | bytes 208904 | tf_op jit(solution)/shard_map/ppermute | solution.py:259
  142.0 1.2 collective-permute-start.15
  143.8 1.8 collective-permute-done.14
  145.5 2.0 collective-permute-done.15
  148.3 0.8 collective-permute-start.18
  149.1 2.7 %collective-permute-start.17 = (f32[128,128]{1,0:T(8,128)S(1)}, f32[128,128]{1,0:T(8,128)S(1)}, u32[]{:S(2)}, u32[]{:S(2)}) collective-permute-start(f32[128,128]{1,0:T(8,128)S(1)} %fusion.1.l0.l), channel_id=1, source_target_pairs={{0,8},{4,12},{8,0},{12,4},{1,9},{5,13},{9,1},{13,5},{2,10},{6,14},... | collective-permute-start | bytes 196616 | tf_op jit(solution)/shard_map/ppermute | solution.py:259
  155.6 1.4 components_keep.5
  157.5 17.4 %all_to_all.43 = f32[32,17,1,128]{3,2,1,0:T(1,128)S(1)} all-to-all(f32[32,17,1,128]{3,2,1,0:T(1,128)S(1)} %pad_maximum_fusion.2), channel_id=1, replica_groups=mesh['z'=8,'c'=2,'x'=4,'y'=4] {'z','y'}, dimensions={0} | all-to-all | bytes 557056 | tf_op jit(solution)/shard_map/all_to_all | solution.py:295
  175.1 16.0 %all_to_all.44 = f32[32,16,128]{2,1,0:T(8,128)S(1)} all-to-all(f32[32,16,128]{2,1,0:T(8,128)S(1)} %broadcast_in_dim.22), channel_id=1, replica_groups=mesh['z'=8,'c'=2,'x'=4,'y'=4] {'z','y'}, dimensions={0} | all-to-all | bytes 524288 | tf_op jit(solution)/shard_map/all_to_all | solution.py:264
  191.1 1.5 loadings_own.5
  193.2 2.8 %collective-permute-start.21 = (f32[136,128]{1,0:T(8,128)S(1)}, f32[136,128]{1,0:T(8,128)S(1)}, u32[]{:S(2)}, u32[]{:S(2)}) collective-permute-start(f32[136,128]{1,0:T(8,128)S(1)} %loadings_other.21), channel_id=1, source_target_pairs={{0,8},{4,12},{8,0},{12,4},{1,9},{5,13},{9,1},{13,5},{2,10},{6,14},... | collective-permute-start | bytes 208904 | tf_op jit(solution)/shard_map/ppermute | solution.py:259
  197.6 0.9 collective-permute-start.23
  199.3 1.5 collective-permute-done.22
  200.8 2.4 %collective-permute-done.23 = f32[136,128]{1,0:T(8,128)S(1)} collective-permute-done((f32[136,128]{1,0:T(8,128)S(1)}, f32[136,128]{1,0:T(8,128)S(1)}, u32[]{:S(2)}, u32[]{:S(2)}) %collective-permute-start.23) | collective-permute-done | bytes 69664 | tf_op jit(solution)/shard_map/ppermute | solution.py:259
  203.2 1.1 broadcast_in_dim.23
  204.3 3.7 %all-to-all-start.7 = ((f32[16,128,128]{2,1,0:T(8,128)}), f32[16,128,128]{2,1,0:T(8,128)S(1)}, u32[]{:S(2)}, u32[]{:S(2)}) async-start(f32[16,128,128]{2,1,0:T(8,128)} %broadcast_in_dim.23), calls=%async_computation.7 | async-start | bytes 2097152 | tf_op jit(solution)/shard_map/all_to_all | solution.py:264
  208.8 15.6 %all-to-all-done.7 = f32[16,128,128]{2,1,0:T(8,128)S(1)} async-done(((f32[16,128,128]{2,1,0:T(8,128)}), f32[16,128,128]{2,1,0:T(8,128)S(1)}, u32[]{:S(2)}, u32[]{:S(2)}) %all-to-all-start.7) | async-done | bytes 1048608 | tf_op jit(solution)/shard_map/all_to_all | solution.py:264
  224.3 1.0 copy.40
  (102 shorter events, 23.7 us)
Async XLA Ops:
  0.6 1.7 copy-start.2
  7.3 29.9 %collective-permute-start.1 = (f32[128,1024]{1,0:T(8,128)}, f32[128,1024]{1,0:T(8,128)S(1)}, u32[]{:S(2)}, u32[]{:S(2)}) collective-permute-start(f32[128,1024]{1,0:T(8,128)} %get-tuple-element.62), channel_id=1, source_target_pairs={{0,8},{4,12},{8,0},{12,4},{1,9},{5,13},{9,1},{13,5},{2,10},{6,14},... | collective-permute-start | bytes 1572872 | tf_op jit(solution)/shard_map/ppermute | solution.py:259
  12.8 24.9 %collective-permute-start = (f32[128,1024]{1,0:T(8,128)}, f32[128,1024]{1,0:T(8,128)S(1)}, u32[]{:S(2)}, u32[]{:S(2)}) collective-permute-start(f32[128,1024]{1,0:T(8,128)} %get-tuple-element.61), channel_id=1, source_target_pairs={{0,4},{4,0},{8,12},{12,8},{1,5},{5,1},{9,13},{13,9},{2,6},{6,2},{1... | collective-permute-start | bytes 1572872 | tf_op jit(solution)/shard_map/ppermute | solution.py:259
  15.9 1.3 copy-start
  17.3 21.0 %collective-permute-start.2 = (f32[128,1024]{1,0:T(8,128)}, f32[128,1024]{1,0:T(8,128)S(1)}, u32[]{:S(2)}, u32[]{:S(2)}) collective-permute-start(f32[128,1024]{1,0:T(8,128)} %get-tuple-element.63), channel_id=1, source_target_pairs={{0,12},{4,8},{8,4},{12,0},{1,13},{5,9},{9,5},{13,1},{2,14},{6,10},... | collective-permute-start | bytes 1572872 | tf_op jit(solution)/shard_map/ppermute | solution.py:259
  17.8 1.6 copy-start.1
  19.4 2.2 copy-start.3
  23.2 13.4 %all-to-all-start = ((f32[4,256,128]{2,1,0:T(8,128)}), f32[4,256,128]{2,1,0:T(8,128)S(1)}, u32[]{:S(2)}, u32[]{:S(2)}) async-start(f32[4,256,128]{2,1,0:T(8,128)} %broadcast_in_dim.16), calls=%async_computation | async-start | bytes 1048576 | tf_op jit(solution)/shard_map/all_to_all | solution.py:264
  38.8 1.6 collective-permute-start.3
  41.5 22.3 %all-to-all-start.1 = ((f32[32,17,1,128]{3,2,1,0:T(1,128)}), f32[32,17,1,128]{3,2,1,0:T(1,128)S(1)}, u32[]{:S(2)}, u32[]{:S(2)}) async-start(f32[32,17,1,128]{3,2,1,0:T(1,128)} %pad_maximum_fusion), calls=%async_computation.1 | async-start | bytes 557056 | tf_op jit(solution)/shard_map/all_to_all | solution.py:295
  80.0 1.5 collective-permute-start.4
  82.0 6.1 %collective-permute-start.5 = (f32[136,128]{1,0:T(8,128)S(1)}, f32[136,128]{1,0:T(8,128)S(1)}, u32[]{:S(2)}, u32[]{:S(2)}) collective-permute-start(f32[136,128]{1,0:T(8,128)S(1)} %loadings_other.13), channel_id=1, source_target_pairs={{0,8},{4,12},{8,0},{12,4},{1,9},{5,13},{9,1},{13,5},{2,10},{6,14},... | collective-permute-start | bytes 208904 | tf_op jit(solution)/shard_map/ppermute | solution.py:259
  85.3 4.4 %collective-permute-start.6 = (f32[136,128]{1,0:T(8,128)S(1)}, f32[136,128]{1,0:T(8,128)S(1)}, u32[]{:S(2)}, u32[]{:S(2)}) collective-permute-start(f32[136,128]{1,0:T(8,128)S(1)} %loadings_other.14), channel_id=1, source_target_pairs={{0,4},{4,0},{8,12},{12,8},{1,5},{5,1},{9,13},{13,9},{2,6},{6,2},{1... | collective-permute-start | bytes 208904 | tf_op jit(solution)/shard_map/ppermute | solution.py:259
  86.5 5.6 %collective-permute-start.7 = (f32[136,128]{1,0:T(8,128)S(1)}, f32[136,128]{1,0:T(8,128)S(1)}, u32[]{:S(2)}, u32[]{:S(2)}) collective-permute-start(f32[136,128]{1,0:T(8,128)S(1)} %loadings_other.15), channel_id=1, source_target_pairs={{0,12},{4,8},{8,4},{12,0},{1,13},{5,9},{9,5},{13,1},{2,14},{6,10},... | collective-permute-start | bytes 208904 | tf_op jit(solution)/shard_map/ppermute | solution.py:259
  92.1 4.7 %collective-permute-start.8 = (f32[128,128]{1,0:T(8,128)S(1)}, f32[128,128]{1,0:T(8,128)S(1)}, u32[]{:S(2)}, u32[]{:S(2)}) collective-permute-start(f32[128,128]{1,0:T(8,128)S(1)} %fusion.2.l0.l), channel_id=1, source_target_pairs={{0,4},{4,0},{8,12},{12,8},{1,5},{5,1},{9,13},{13,9},{2,6},{6,2},{1... | collective-permute-start | bytes 196616 | tf_op jit(solution)/shard_map/ppermute | solution.py:259
  92.4 5.5 %collective-permute-start.10 = (f32[128,128]{1,0:T(8,128)S(1)}, f32[128,128]{1,0:T(8,128)S(1)}, u32[]{:S(2)}, u32[]{:S(2)}) collective-permute-start(f32[128,128]{1,0:T(8,128)S(1)} %fusion.2.l0.l), channel_id=1, source_target_pairs={{0,12},{4,8},{8,4},{12,0},{1,13},{5,9},{9,5},{13,1},{2,14},{6,10},... | collective-permute-start | bytes 196616 | tf_op jit(solution)/shard_map/ppermute | solution.py:259
  93.6 5.8 %collective-permute-start.9 = (f32[128,128]{1,0:T(8,128)S(1)}, f32[128,128]{1,0:T(8,128)S(1)}, u32[]{:S(2)}, u32[]{:S(2)}) collective-permute-start(f32[128,128]{1,0:T(8,128)S(1)} %fusion.2.l0.l), channel_id=1, source_target_pairs={{0,8},{4,12},{8,0},{12,4},{1,9},{5,13},{9,1},{13,5},{2,10},{6,14},... | collective-permute-start | bytes 196616 | tf_op jit(solution)/shard_map/ppermute | solution.py:259
  100.0 1.6 collective-permute-start.11
  135.6 1.5 collective-permute-start.12
  137.6 6.1 %collective-permute-start.13 = (f32[136,128]{1,0:T(8,128)S(1)}, f32[136,128]{1,0:T(8,128)S(1)}, u32[]{:S(2)}, u32[]{:S(2)}) collective-permute-start(f32[136,128]{1,0:T(8,128)S(1)} %loadings_other.17), channel_id=1, source_target_pairs={{0,8},{4,12},{8,0},{12,4},{1,9},{5,13},{9,1},{13,5},{2,10},{6,14},... | collective-permute-start | bytes 208904 | tf_op jit(solution)/shard_map/ppermute | solution.py:259
  140.9 4.6 %collective-permute-start.14 = (f32[136,128]{1,0:T(8,128)S(1)}, f32[136,128]{1,0:T(8,128)S(1)}, u32[]{:S(2)}, u32[]{:S(2)}) collective-permute-start(f32[136,128]{1,0:T(8,128)S(1)} %loadings_other.18), channel_id=1, source_target_pairs={{0,4},{4,0},{8,12},{12,8},{1,5},{5,1},{9,13},{13,9},{2,6},{6,2},{1... | collective-permute-start | bytes 208904 | tf_op jit(solution)/shard_map/ppermute | solution.py:259
  142.0 5.6 %collective-permute-start.15 = (f32[136,128]{1,0:T(8,128)S(1)}, f32[136,128]{1,0:T(8,128)S(1)}, u32[]{:S(2)}, u32[]{:S(2)}) collective-permute-start(f32[136,128]{1,0:T(8,128)S(1)} %loadings_other.19), channel_id=1, source_target_pairs={{0,12},{4,8},{8,4},{12,0},{1,13},{5,9},{9,5},{13,1},{2,14},{6,10},... | collective-permute-start | bytes 208904 | tf_op jit(solution)/shard_map/ppermute | solution.py:259
  147.6 4.9 %collective-permute-start.16 = (f32[128,128]{1,0:T(8,128)S(1)}, f32[128,128]{1,0:T(8,128)S(1)}, u32[]{:S(2)}, u32[]{:S(2)}) collective-permute-start(f32[128,128]{1,0:T(8,128)S(1)} %fusion.1.l0.l), channel_id=1, source_target_pairs={{0,4},{4,0},{8,12},{12,8},{1,5},{5,1},{9,13},{13,9},{2,6},{6,2},{1... | collective-permute-start | bytes 196616 | tf_op jit(solution)/shard_map/ppermute | solution.py:259
  148.3 5.5 %collective-permute-start.18 = (f32[128,128]{1,0:T(8,128)S(1)}, f32[128,128]{1,0:T(8,128)S(1)}, u32[]{:S(2)}, u32[]{:S(2)}) collective-permute-start(f32[128,128]{1,0:T(8,128)S(1)} %fusion.1.l0.l), channel_id=1, source_target_pairs={{0,12},{4,8},{8,4},{12,0},{1,13},{5,9},{9,5},{13,1},{2,14},{6,10},... | collective-permute-start | bytes 196616 | tf_op jit(solution)/shard_map/ppermute | solution.py:259
  149.1 5.8 %collective-permute-start.17 = (f32[128,128]{1,0:T(8,128)S(1)}, f32[128,128]{1,0:T(8,128)S(1)}, u32[]{:S(2)}, u32[]{:S(2)}) collective-permute-start(f32[128,128]{1,0:T(8,128)S(1)} %fusion.1.l0.l), channel_id=1, source_target_pairs={{0,8},{4,12},{8,0},{12,4},{1,9},{5,13},{9,1},{13,5},{2,10},{6,14},... | collective-permute-start | bytes 196616 | tf_op jit(solution)/shard_map/ppermute | solution.py:259
  155.5 1.6 collective-permute-start.19
  191.1 1.5 collective-permute-start.20
  193.2 6.1 %collective-permute-start.21 = (f32[136,128]{1,0:T(8,128)S(1)}, f32[136,128]{1,0:T(8,128)S(1)}, u32[]{:S(2)}, u32[]{:S(2)}) collective-permute-start(f32[136,128]{1,0:T(8,128)S(1)} %loadings_other.21), channel_id=1, source_target_pairs={{0,8},{4,12},{8,0},{12,4},{1,9},{5,13},{9,1},{13,5},{2,10},{6,14},... | collective-permute-start | bytes 208904 | tf_op jit(solution)/shard_map/ppermute | solution.py:259
  196.4 4.4 %collective-permute-start.22 = (f32[136,128]{1,0:T(8,128)S(1)}, f32[136,128]{1,0:T(8,128)S(1)}, u32[]{:S(2)}, u32[]{:S(2)}) collective-permute-start(f32[136,128]{1,0:T(8,128)S(1)} %loadings_other.22), channel_id=1, source_target_pairs={{0,4},{4,0},{8,12},{12,8},{1,5},{5,1},{9,13},{13,9},{2,6},{6,2},{1... | collective-permute-start | bytes 208904 | tf_op jit(solution)/shard_map/ppermute | solution.py:259
  197.6 5.6 %collective-permute-start.23 = (f32[136,128]{1,0:T(8,128)S(1)}, f32[136,128]{1,0:T(8,128)S(1)}, u32[]{:S(2)}, u32[]{:S(2)}) collective-permute-start(f32[136,128]{1,0:T(8,128)S(1)} %loadings_other.23), channel_id=1, source_target_pairs={{0,12},{4,8},{8,4},{12,0},{1,13},{5,9},{9,5},{13,1},{2,14},{6,10},... | collective-permute-start | bytes 208904 | tf_op jit(solution)/shard_map/ppermute | solution.py:259
  204.3 20.0 %all-to-all-start.7 = ((f32[16,128,128]{2,1,0:T(8,128)}), f32[16,128,128]{2,1,0:T(8,128)S(1)}, u32[]{:S(2)}, u32[]{:S(2)}) async-start(f32[16,128,128]{2,1,0:T(8,128)} %broadcast_in_dim.23), calls=%async_computation.7 | async-start | bytes 2097152 | tf_op jit(solution)/shard_map/all_to_all | solution.py:264

commit v3 on v2

--- a/solution.py
+++ b/solution.py
@@ -53,7 +53,7 @@
         out_specs=[pl.BlockSpec(memory_space=VMEM)] * (len(outs) + len(kept)),
         scratch_shapes=list(scratch),
         input_output_aliases=aliases or {},
-        compiler_params=pltpu.CompilerParams(vmem_limit_bytes=16 << 20),
+        compiler_params=pltpu.CompilerParams(vmem_limit_bytes=8 << 20),
         cost_estimate=pl.CostEstimate(flops=cost, bytes_accessed=cost, transcendentals=0),
         name=name,
     )(*ins)
@@ -102,13 +102,13 @@
         in_specs=[pl.BlockSpec(memory_space=VMEM)],
         out_specs=[pl.BlockSpec(memory_space=VMEM)] * 2,
         scratch_shapes=[pltpu.VMEM((LANES, LANES), F32)] * 4,
-        compiler_params=pltpu.CompilerParams(vmem_limit_bytes=16 << 20),
+        compiler_params=pltpu.CompilerParams(vmem_limit_bytes=8 << 20),
         cost_estimate=pl.CostEstimate(flops=1 << 20, bytes_accessed=12 << 20, transcendentals=0),
         name="bands",
     )(resolution)
 
 
-def smear_kernel(blocks, d, idx_ref, field_ref, bh_ref, bl_ref, out, token, _, __, ___, vh, vl, uh, ul):
+def smear_kernel(blocks, d, idx_ref, field_ref, bh_ref, bl_ref, out, token, _, __, vh, vl, uh, ul):
     token[...] = jnp.zeros(token.shape, F32)
     rows = field_ref.shape[0]
     per = blocks // 4
@@ -169,7 +169,7 @@
         rows * width * LANES,
         scratch,
         1,
-        {1: 2, 2: 3, 3: 4},
+        {2: 2, 3: 3},
     )
 
 
@@ -259,8 +259,8 @@
     return lax.ppermute(x, axis, [(i, i ^ distance) for i in range(size)])
 
 
-def spread(x, axes, copies):
-    y = jnp.broadcast_to(x[None], (copies,) + x.shape)
+def spread(x, axes, copies, zero=0.0):
+    y = jnp.broadcast_to(x[None], (copies,) + x.shape) + zero
     return lax.all_to_all(y, axes, 0, 0).reshape((-1,) + x.shape[1:])
 
 
@@ -270,13 +270,12 @@
     comps = components_start.shape[0]
     idx = jnp.stack([xi, ci]).astype(jnp.int32)
     bh, bl = make_bands(resolution)
-    field = measured
     xs = [None] * 4
     for d in (2, 1, 3, 0):
-        xs[d], zero, field, bh, bl = smear(d, idx, field, bh, bl)
+        xs[d], zero, bh, bl = smear(d, idx, measured, bh, bl)
         if d:
             xs[d] = swap(xs[d], "x", d)
-    start = spread((components_start + zero[0, 0]).T, "y", 4)
+    start = spread(components_start.T, "y", 4, zero[0, 0])
     half = start.shape[0] // 2
     mine = lax.dynamic_slice_in_dim(start, ci * half, half)
     theirs = lax.dynamic_slice_in_dim(start, (1 - ci) * half, half)
@@ -286,7 +285,7 @@
     part = half // group
     piece = lax.dynamic_slice_in_dim(mine, (zi * 4 + yi) * part, part)
     for step in range(ITERS):
-        keep, send = components_part(xs, ls, mine, theirs, (0, 1, 3, 2) if step else (0, 2, 1, 3))
+        keep, send = components_part(xs, ls, mine, theirs, (0, 2, 1, 3))
         both = keep + swap(send, "c", 1)
         totals = jnp.sum(both[half:], axis=0)
         packed = jnp.concatenate(

time: 226 us -> 226 us (level)
    unnamed x11 -> x8, local copies, waits for them, and re-layouts: 6.36 us -> 4.4 us
  transfers between devices with their start and end apart: 27 -> 27, of which waited for: 22 -> 21; matrix products, arithmetic and copies ran while one was open for 2% -> 2% of each run, Pallas kernels for 11% -> 11%
where the time goes in v3:
time: 226 us; the launch traced here: 225 us
  blocking collectives  82.8 us (37%)
  waiting for transfers between devices  52.7 us (23%)
  starting transfers between devices  43.7 us (19%)
  Pallas kernels  31.8 us (14%)
  local copies, waits for them, and re-layouts  9.1 us (4%)
  other arithmetic  3.76 us (2%)
    all_to_all x3, blocking collectives, spread(): return lax.all_to_all(y, axes, 0, 0).reshape((-1,) + x.shape[1:])  48 us
    all_to_all x2, blocking collectives, local(): total = jnp.sum(lax.all_to_all(packed, ('z', 'y'), 0, 0), axis=0)[:, 0]  34.8 us
    pallas_call x34, Pallas kernels, call(): pl.pallas_call(kernel, out_shape=[jax.ShapeDtypeStruct(o, F32) for o in o...  29.5 us
    ppermute x24, starting transfers between devices, swap(): return lax.ppermute(x, axis, [(i, i ^ distance) for i in range(size)])  26.1 us
    all_to_all x2, waiting for transfers between devices, spread(): return lax.all_to_all(y, axes, 0, 0).reshape((-1,) + x.shape[1:])  23.7 us
    ppermute x24, waiting for transfers between devices, swap(): return lax.ppermute(x, axis, [(i, i ^ distance) for i in range(size)])  16.1 us
    all_to_all x1, waiting for transfers between devices, local(): total = jnp.sum(lax.all_to_all(packed, ('z', 'y'), 0, 0), axis=0)[:, 0]  12.9 us
    all_to_all x1, starting transfers between devices, local(): total = jnp.sum(lax.all_to_all(packed, ('z', 'y'), 0, 0), axis=0)[:, 0]  9.47 us
  transfers between devices with their start and end apart: 27, of which 21 were waited for; matrix products, arithmetic and copies ran while one was open for 2% of the time, Pallas kernels for 11%

profile of v3, /device:TPU:32, one launch (start us, length us, event | category | flops | bytes accessed | tf_op | source)
XLA Modules:
  0.0 225.1 jit_solution(16947811671378834615)
XLA Ops:
  0.6 1.1 copy-done.1
  1.7 2.3 %bands.1 = (bf16[4352,256]{1,0:T(8,128)(2,1)S(1)}, bf16[4352,256]{1,0:T(8,128)(2,1)S(1)}) custom-call(f32[33,4096]{1,0:T(8,128)S(1)} %copy-done.1), custom_call_target="tpu_custom_call" | custom-call | flops 1048576 | bytes 12582912 | tf_op jit(solution)/shard_map/bands/pallas_call | solution.py:99
  4.2 1.6 copy-done
  5.7 2.3 %smear.4 = (f32[128,1024]{1,0:T(8,128)S(1)}, f32[8,128]{1,0:T(8,128)}, bf16[4352,256]{1,0:T(8,128)(2,1)S(1)}, bf16[4352,256]{1,0:T(8,128)(2,1)S(1)}) custom-call(s32[2]{0:T(128)S(1)} %pad_add_fusion.idx_ref, f32[128,4096]{1,0:T(8,128)S(1)} %copy-done, bf16[4352,256]{1,0:T(8,128)(2,1)S(1)} %get-tuple-element.45.bh_ref, ...), custom_call_target="tpu_custom_call", output_to_operand_aliasing={{2}: (2, {}), {3}: (3, {})} | custom-call | flops 1024 | bytes 1024 | tf_op jit(solution)/shard_map/smear/pallas_call | solution.py:49
  8.0 3.0 %collective-permute-start.1 = (f32[128,1024]{1,0:T(8,128)S(1)}, f32[128,1024]{1,0:T(8,128)S(1)}, u32[]{:S(2)}, u32[]{:S(2)}) collective-permute-start(f32[128,1024]{1,0:T(8,128)S(1)} %get-tuple-element.56), channel_id=1, source_target_pairs={{0,8},{4,12},{8,0},{12,4},{1,9},{5,13},{9,1},{13,5},{2,10},{6,14},... | collective-permute-start | bytes 1572872 | tf_op jit(solution)/shard_map/ppermute | solution.py:259
  11.0 2.3 %smear.5 = (f32[128,1024]{1,0:T(8,128)S(1)}, f32[8,128]{1,0:T(8,128)}, bf16[4352,256]{1,0:T(8,128)(2,1)S(1)}, bf16[4352,256]{1,0:T(8,128)(2,1)S(1)}) custom-call(s32[2]{0:T(128)S(1)} %pad_add_fusion.idx_ref, f32[128,4096]{1,0:T(8,128)S(1)} %copy-done, bf16[4352,256]{1,0:T(8,128)(2,1)S(1)} %get-tuple-element.47.bh_ref, ...), custom_call_target="tpu_custom_call", output_to_operand_aliasing={{2}: (2, {}), {3}: (3, {})} | custom-call | flops 1024 | bytes 1024 | tf_op jit(solution)/shard_map/smear/pallas_call | solution.py:49
  13.9 2.5 %smear.6 = (f32[128,1024]{1,0:T(8,128)}, f32[8,128]{1,0:T(8,128)}, bf16[4352,256]{1,0:T(8,128)(2,1)S(1)}, bf16[4352,256]{1,0:T(8,128)(2,1)S(1)}) custom-call(s32[2]{0:T(128)S(1)} %pad_add_fusion.idx_ref, f32[128,4096]{1,0:T(8,128)S(1)} %copy-done, bf16[4352,256]{1,0:T(8,128)(2,1)S(1)} %get-tuple-element.49.bh_ref, ...), custom_call_target="tpu_custom_call", output_to_operand_aliasing={{2}: (2, {}), {3}: (3, {})} | custom-call | flops 1024 | bytes 1024 | tf_op jit(solution)/shard_map/smear/pallas_call | solution.py:49
  17.0 1.7 smear.7
  20.8 4.5 %all-to-all-start = ((f32[4,256,128]{2,1,0:T(8,128)}), f32[4,256,128]{2,1,0:T(8,128)}, u32[]{:S(2)}, u32[]{:S(2)}) async-start(f32[4,256,128]{2,1,0:T(8,128)} %broadcast_in_dim.16), calls=%async_computation | async-start | bytes 1048576 | tf_op jit(solution)/shard_map/all_to_all | solution.py:264
  25.3 1.0 constant_dynamic-slice_fusion.3
  26.3 8.1 %all-to-all-done = f32[4,256,128]{2,1,0:T(8,128)} async-done(((f32[4,256,128]{2,1,0:T(8,128)}), f32[4,256,128]{2,1,0:T(8,128)}, u32[]{:S(2)}, u32[]{:S(2)}) %all-to-all-start) | async-done | bytes 524320 | tf_op jit(solution)/shard_map/all_to_all | solution.py:264
  34.3 1.1 constant_dynamic-slice_fusion
  37.6 1.4 components_keep.3
  39.3 1.0 pad_maximum_fusion
  40.2 9.5 %all-to-all-start.1 = ((f32[32,17,1,128]{3,2,1,0:T(1,128)}), f32[32,17,1,128]{3,2,1,0:T(1,128)S(1)}, u32[]{:S(2)}, u32[]{:S(2)}) async-start(f32[32,17,1,128]{3,2,1,0:T(1,128)} %pad_maximum_fusion), calls=%async_computation.1 | async-start | bytes 557056 | tf_op jit(solution)/shard_map/all_to_all | solution.py:294
  49.7 12.9 %all-to-all-done.1 = f32[32,17,1,128]{3,2,1,0:T(1,128)S(1)} async-done(((f32[32,17,1,128]{3,2,1,0:T(1,128)}), f32[32,17,1,128]{3,2,1,0:T(1,128)S(1)}, u32[]{:S(2)}, u32[]{:S(2)}) %all-to-all-start.1) | async-done | bytes 278560 | tf_op jit(solution)/shard_map/all_to_all | solution.py:294
  63.6 16.0 %all_to_all.40 = f32[32,16,128]{2,1,0:T(8,128)S(1)} all-to-all(f32[32,16,128]{2,1,0:T(8,128)S(1)} %broadcast_in_dim.18), channel_id=1, replica_groups=mesh['z'=8,'c'=2,'x'=4,'y'=4] {'z','y'}, dimensions={0} | all-to-all | bytes 524288 | tf_op jit(solution)/shard_map/all_to_all | solution.py:264
  79.6 1.5 loadings_own.3
  81.6 2.6 %collective-permute-start.5 = (f32[136,128]{1,0:T(8,128)S(1)}, f32[136,128]{1,0:T(8,128)S(1)}, u32[]{:S(2)}, u32[]{:S(2)}) collective-permute-start(f32[136,128]{1,0:T(8,128)S(1)} %loadings_other.13), channel_id=1, source_target_pairs={{0,8},{4,12},{8,0},{12,4},{1,9},{5,13},{9,1},{13,5},{2,10},{6,14},... | collective-permute-start | bytes 208904 | tf_op jit(solution)/shard_map/ppermute | solution.py:259
  85.9 1.1 collective-permute-start.7
  87.8 1.4 collective-permute-done.6
  89.1 2.4 %collective-permute-done.7 = f32[136,128]{1,0:T(8,128)S(1)} collective-permute-done((f32[136,128]{1,0:T(8,128)S(1)}, f32[136,128]{1,0:T(8,128)S(1)}, u32[]{:S(2)}, u32[]{:S(2)}) %collective-permute-start.7) | collective-permute-done | bytes 69664 | tf_op jit(solution)/shard_map/ppermute | solution.py:259
  91.6 1.3 collective-permute-start.9
  93.5 2.2 collective-permute-start.10
  96.3 1.2 collective-permute-done.9.l2.l
  99.7 1.4 components_keep.4
  101.6 17.4 %all_to_all.41 = f32[32,17,1,128]{3,2,1,0:T(1,128)S(1)} all-to-all(f32[32,17,1,128]{3,2,1,0:T(1,128)S(1)} %pad_maximum_fusion.1), channel_id=1, replica_groups=mesh['z'=8,'c'=2,'x'=4,'y'=4] {'z','y'}, dimensions={0} | all-to-all | bytes 557056 | tf_op jit(solution)/shard_map/all_to_all | solution.py:294
  119.2 16.0 %all_to_all.42 = f32[32,16,128]{2,1,0:T(8,128)S(1)} all-to-all(f32[32,16,128]{2,1,0:T(8,128)S(1)} %broadcast_in_dim.20), channel_id=1, replica_groups=mesh['z'=8,'c'=2,'x'=4,'y'=4] {'z','y'}, dimensions={0} | all-to-all | bytes 524288 | tf_op jit(solution)/shard_map/all_to_all | solution.py:264
  135.2 1.5 loadings_own.4
  137.2 1.4 collective-permute-start.13
  139.1 2.1 collective-permute-start.14
  141.7 1.1 collective-permute-start.15
  144.4 2.9 %collective-permute-done.15 = f32[136,128]{1,0:T(8,128)S(1)} collective-permute-done((f32[136,128]{1,0:T(8,128)S(1)}, f32[136,128]{1,0:T(8,128)S(1)}, u32[]{:S(2)}, u32[]{:S(2)}) %collective-permute-start.15) | collective-permute-done | bytes 69664 | tf_op jit(solution)/shard_map/ppermute | solution.py:259
  147.5 1.8 collective-permute-start.16
  149.3 2.2 collective-permute-start.18
  152.1 1.2 collective-permute-done.17.l2.l
  155.5 1.4 components_keep.5
  157.4 17.4 %all_to_all.43 = f32[32,17,1,128]{3,2,1,0:T(1,128)S(1)} all-to-all(f32[32,17,1,128]{3,2,1,0:T(1,128)S(1)} %pad_maximum_fusion.2), channel_id=1, replica_groups=mesh['z'=8,'c'=2,'x'=4,'y'=4] {'z','y'}, dimensions={0} | all-to-all | bytes 557056 | tf_op jit(solution)/shard_map/all_to_all | solution.py:294
  175.0 16.0 %all_to_all.44 = f32[32,16,128]{2,1,0:T(8,128)S(1)} all-to-all(f32[32,16,128]{2,1,0:T(8,128)S(1)} %broadcast_in_dim.22), channel_id=1, replica_groups=mesh['z'=8,'c'=2,'x'=4,'y'=4] {'z','y'}, dimensions={0} | all-to-all | bytes 524288 | tf_op jit(solution)/shard_map/all_to_all | solution.py:264
  191.0 1.5 loadings_own.5
  193.1 1.1 collective-permute-start.21
  194.6 2.2 collective-permute-start.22
  197.3 1.1 collective-permute-start.23
  200.3 2.6 %collective-permute-done.23 = f32[136,128]{1,0:T(8,128)S(1)} collective-permute-done((f32[136,128]{1,0:T(8,128)S(1)}, f32[136,128]{1,0:T(8,128)S(1)}, u32[]{:S(2)}, u32[]{:S(2)}) %collective-permute-start.23) | collective-permute-done | bytes 69664 | tf_op jit(solution)/shard_map/ppermute | solution.py:259
  203.0 1.1 broadcast_in_dim.23
  204.1 3.7 %all-to-all-start.7 = ((f32[16,128,128]{2,1,0:T(8,128)}), f32[16,128,128]{2,1,0:T(8,128)S(1)}, u32[]{:S(2)}, u32[]{:S(2)}) async-start(f32[16,128,128]{2,1,0:T(8,128)} %broadcast_in_dim.23), calls=%async_computation.7 | async-start | bytes 2097152 | tf_op jit(solution)/shard_map/all_to_all | solution.py:264
  208.5 15.6 %all-to-all-done.7 = f32[16,128,128]{2,1,0:T(8,128)S(1)} async-done(((f32[16,128,128]{2,1,0:T(8,128)}), f32[16,128,128]{2,1,0:T(8,128)S(1)}, u32[]{:S(2)}, u32[]{:S(2)}) %all-to-all-start.7) | async-done | bytes 1048608 | tf_op jit(solution)/shard_map/all_to_all | solution.py:264
  224.2 1.0 copy.30
  (99 shorter events, 24.7 us)
Async XLA Ops:
  0.6 1.1 copy-start.1
  4.2 1.6 copy-start
  8.0 27.9 %collective-permute-start.1 = (f32[128,1024]{1,0:T(8,128)S(1)}, f32[128,1024]{1,0:T(8,128)S(1)}, u32[]{:S(2)}, u32[]{:S(2)}) collective-permute-start(f32[128,1024]{1,0:T(8,128)S(1)} %get-tuple-element.56), channel_id=1, source_target_pairs={{0,8},{4,12},{8,0},{12,4},{1,9},{5,13},{9,1},{13,5},{2,10},{6,14},... | collective-permute-start | bytes 1572872 | tf_op jit(solution)/shard_map/ppermute | solution.py:259
  13.3 23.1 %collective-permute-start = (f32[128,1024]{1,0:T(8,128)S(1)}, f32[128,1024]{1,0:T(8,128)S(1)}, u32[]{:S(2)}, u32[]{:S(2)}) collective-permute-start(f32[128,1024]{1,0:T(8,128)S(1)} %get-tuple-element.55), channel_id=1, source_target_pairs={{0,4},{4,0},{8,12},{12,8},{1,5},{5,1},{9,13},{13,9},{2,6},{6,2},{1... | collective-permute-start | bytes 1572872 | tf_op jit(solution)/shard_map/ppermute | solution.py:259
  16.4 20.5 %collective-permute-start.2 = (f32[128,1024]{1,0:T(8,128)}, f32[128,1024]{1,0:T(8,128)S(1)}, u32[]{:S(2)}, u32[]{:S(2)}) collective-permute-start(f32[128,1024]{1,0:T(8,128)} %get-tuple-element.57), channel_id=1, source_target_pairs={{0,12},{4,8},{8,4},{12,0},{1,13},{5,9},{9,5},{13,1},{2,14},{6,10},... | collective-permute-start | bytes 1572872 | tf_op jit(solution)/shard_map/ppermute | solution.py:259
  17.0 2.3 %copy-start.2 = (f32[128,256]{1,0:T(8,128)S(1)}, f32[128,256]{1,0:T(8,128)}, u32[]{:S(2)}) copy-start(f32[128,256]{1,0:T(8,128)} %param.7) | copy-start | bytes 393220
  20.8 13.5 %all-to-all-start = ((f32[4,256,128]{2,1,0:T(8,128)}), f32[4,256,128]{2,1,0:T(8,128)}, u32[]{:S(2)}, u32[]{:S(2)}) async-start(f32[4,256,128]{2,1,0:T(8,128)} %broadcast_in_dim.16), calls=%async_computation | async-start | bytes 1048576 | tf_op jit(solution)/shard_map/all_to_all | solution.py:264
  37.5 1.6 collective-permute-start.3
  40.2 22.4 %all-to-all-start.1 = ((f32[32,17,1,128]{3,2,1,0:T(1,128)}), f32[32,17,1,128]{3,2,1,0:T(1,128)S(1)}, u32[]{:S(2)}, u32[]{:S(2)}) async-start(f32[32,17,1,128]{3,2,1,0:T(1,128)} %pad_maximum_fusion), calls=%async_computation.1 | async-start | bytes 557056 | tf_op jit(solution)/shard_map/all_to_all | solution.py:294
  79.6 1.5 collective-permute-start.4
  81.6 6.2 %collective-permute-start.5 = (f32[136,128]{1,0:T(8,128)S(1)}, f32[136,128]{1,0:T(8,128)S(1)}, u32[]{:S(2)}, u32[]{:S(2)}) collective-permute-start(f32[136,128]{1,0:T(8,128)S(1)} %loadings_other.13), channel_id=1, source_target_pairs={{0,8},{4,12},{8,0},{12,4},{1,9},{5,13},{9,1},{13,5},{2,10},{6,14},... | collective-permute-start | bytes 208904 | tf_op jit(solution)/shard_map/ppermute | solution.py:259
  84.7 4.4 %collective-permute-start.6 = (f32[136,128]{1,0:T(8,128)S(1)}, f32[136,128]{1,0:T(8,128)S(1)}, u32[]{:S(2)}, u32[]{:S(2)}) collective-permute-start(f32[136,128]{1,0:T(8,128)S(1)} %loadings_other.14), channel_id=1, source_target_pairs={{0,4},{4,0},{8,12},{12,8},{1,5},{5,1},{9,13},{13,9},{2,6},{6,2},{1... | collective-permute-start | bytes 208904 | tf_op jit(solution)/shard_map/ppermute | solution.py:259
  85.9 5.6 %collective-permute-start.7 = (f32[136,128]{1,0:T(8,128)S(1)}, f32[136,128]{1,0:T(8,128)S(1)}, u32[]{:S(2)}, u32[]{:S(2)}) collective-permute-start(f32[136,128]{1,0:T(8,128)S(1)} %loadings_other.15), channel_id=1, source_target_pairs={{0,12},{4,8},{8,4},{12,0},{1,13},{5,9},{9,5},{13,1},{2,14},{6,10},... | collective-permute-start | bytes 208904 | tf_op jit(solution)/shard_map/ppermute | solution.py:259
  91.6 5.9 %collective-permute-start.9 = (f32[128,128]{1,0:T(8,128)S(1)}, f32[128,128]{1,0:T(8,128)S(1)}, u32[]{:S(2)}, u32[]{:S(2)}) collective-permute-start(f32[128,128]{1,0:T(8,128)S(1)} %fusion.2.l0.l), channel_id=1, source_target_pairs={{0,8},{4,12},{8,0},{12,4},{1,9},{5,13},{9,1},{13,5},{2,10},{6,14},... | collective-permute-start | bytes 196616 | tf_op jit(solution)/shard_map/ppermute | solution.py:259
  92.9 5.0 %collective-permute-start.8 = (f32[128,128]{1,0:T(8,128)S(1)}, f32[128,128]{1,0:T(8,128)S(1)}, u32[]{:S(2)}, u32[]{:S(2)}) collective-permute-start(f32[128,128]{1,0:T(8,128)S(1)} %fusion.2.l0.l), channel_id=1, source_target_pairs={{0,4},{4,0},{8,12},{12,8},{1,5},{5,1},{9,13},{13,9},{2,6},{6,2},{1... | collective-permute-start | bytes 196616 | tf_op jit(solution)/shard_map/ppermute | solution.py:259
  93.5 5.5 %collective-permute-start.10 = (f32[128,128]{1,0:T(8,128)S(1)}, f32[128,128]{1,0:T(8,128)S(1)}, u32[]{:S(2)}, u32[]{:S(2)}) collective-permute-start(f32[128,128]{1,0:T(8,128)S(1)} %fusion.2.l0.l), channel_id=1, source_target_pairs={{0,12},{4,8},{8,4},{12,0},{1,13},{5,9},{9,5},{13,1},{2,14},{6,10},... | collective-permute-start | bytes 196616 | tf_op jit(solution)/shard_map/ppermute | solution.py:259
  99.6 1.6 collective-permute-start.11
  135.2 1.5 collective-permute-start.12
  137.2 6.3 %collective-permute-start.13 = (f32[136,128]{1,0:T(8,128)S(1)}, f32[136,128]{1,0:T(8,128)S(1)}, u32[]{:S(2)}, u32[]{:S(2)}) collective-permute-start(f32[136,128]{1,0:T(8,128)S(1)} %loadings_other.17), channel_id=1, source_target_pairs={{0,8},{4,12},{8,0},{12,4},{1,9},{5,13},{9,1},{13,5},{2,10},{6,14},... | collective-permute-start | bytes 208904 | tf_op jit(solution)/shard_map/ppermute | solution.py:259
  139.1 5.3 %collective-permute-start.14 = (f32[136,128]{1,0:T(8,128)S(1)}, f32[136,128]{1,0:T(8,128)S(1)}, u32[]{:S(2)}, u32[]{:S(2)}) collective-permute-start(f32[136,128]{1,0:T(8,128)S(1)} %loadings_other.18), channel_id=1, source_target_pairs={{0,4},{4,0},{8,12},{12,8},{1,5},{5,1},{9,13},{13,9},{2,6},{6,2},{1... | collective-permute-start | bytes 208904 | tf_op jit(solution)/shard_map/ppermute | solution.py:259
  141.7 5.6 %collective-permute-start.15 = (f32[136,128]{1,0:T(8,128)S(1)}, f32[136,128]{1,0:T(8,128)S(1)}, u32[]{:S(2)}, u32[]{:S(2)}) collective-permute-start(f32[136,128]{1,0:T(8,128)S(1)} %loadings_other.19), channel_id=1, source_target_pairs={{0,12},{4,8},{8,4},{12,0},{1,13},{5,9},{9,5},{13,1},{2,14},{6,10},... | collective-permute-start | bytes 208904 | tf_op jit(solution)/shard_map/ppermute | solution.py:259
  147.4 5.9 %collective-permute-start.17 = (f32[128,128]{1,0:T(8,128)S(1)}, f32[128,128]{1,0:T(8,128)S(1)}, u32[]{:S(2)}, u32[]{:S(2)}) collective-permute-start(f32[128,128]{1,0:T(8,128)S(1)} %fusion.1.l0.l), channel_id=1, source_target_pairs={{0,8},{4,12},{8,0},{12,4},{1,9},{5,13},{9,1},{13,5},{2,10},{6,14},... | collective-permute-start | bytes 196616 | tf_op jit(solution)/shard_map/ppermute | solution.py:259
  147.5 6.3 %collective-permute-start.16 = (f32[128,128]{1,0:T(8,128)S(1)}, f32[128,128]{1,0:T(8,128)S(1)}, u32[]{:S(2)}, u32[]{:S(2)}) collective-permute-start(f32[128,128]{1,0:T(8,128)S(1)} %fusion.1.l0.l), channel_id=1, source_target_pairs={{0,4},{4,0},{8,12},{12,8},{1,5},{5,1},{9,13},{13,9},{2,6},{6,2},{1... | collective-permute-start | bytes 196616 | tf_op jit(solution)/shard_map/ppermute | solution.py:259
  149.3 5.5 %collective-permute-start.18 = (f32[128,128]{1,0:T(8,128)S(1)}, f32[128,128]{1,0:T(8,128)S(1)}, u32[]{:S(2)}, u32[]{:S(2)}) collective-permute-start(f32[128,128]{1,0:T(8,128)S(1)} %fusion.1.l0.l), channel_id=1, source_target_pairs={{0,12},{4,8},{8,4},{12,0},{1,13},{5,9},{9,5},{13,1},{2,14},{6,10},... | collective-permute-start | bytes 196616 | tf_op jit(solution)/shard_map/ppermute | solution.py:259
  155.4 1.6 collective-permute-start.19
  191.0 1.5 collective-permute-start.20
  193.1 6.6 %collective-permute-start.21 = (f32[136,128]{1,0:T(8,128)S(1)}, f32[136,128]{1,0:T(8,128)S(1)}, u32[]{:S(2)}, u32[]{:S(2)}) collective-permute-start(f32[136,128]{1,0:T(8,128)S(1)} %loadings_other.21), channel_id=1, source_target_pairs={{0,8},{4,12},{8,0},{12,4},{1,9},{5,13},{9,1},{13,5},{2,10},{6,14},... | collective-permute-start | bytes 208904 | tf_op jit(solution)/shard_map/ppermute | solution.py:259
  194.6 5.6 %collective-permute-start.22 = (f32[136,128]{1,0:T(8,128)S(1)}, f32[136,128]{1,0:T(8,128)S(1)}, u32[]{:S(2)}, u32[]{:S(2)}) collective-permute-start(f32[136,128]{1,0:T(8,128)S(1)} %loadings_other.22), channel_id=1, source_target_pairs={{0,4},{4,0},{8,12},{12,8},{1,5},{5,1},{9,13},{13,9},{2,6},{6,2},{1... | collective-permute-start | bytes 208904 | tf_op jit(solution)/shard_map/ppermute | solution.py:259
  197.3 5.6 %collective-permute-start.23 = (f32[136,128]{1,0:T(8,128)S(1)}, f32[136,128]{1,0:T(8,128)S(1)}, u32[]{:S(2)}, u32[]{:S(2)}) collective-permute-start(f32[136,128]{1,0:T(8,128)S(1)} %loadings_other.23), channel_id=1, source_target_pairs={{0,12},{4,8},{8,4},{12,0},{1,13},{5,9},{9,5},{13,1},{2,14},{6,10},... | collective-permute-start | bytes 208904 | tf_op jit(solution)/shard_map/ppermute | solution.py:259
  204.1 20.1 %all-to-all-start.7 = ((f32[16,128,128]{2,1,0:T(8,128)}), f32[16,128,128]{2,1,0:T(8,128)S(1)}, u32[]{:S(2)}, u32[]{:S(2)}) async-start(f32[16,128,128]{2,1,0:T(8,128)} %broadcast_in_dim.23), calls=%async_computation.7 | async-start | bytes 2097152 | tf_op jit(solution)/shard_map/all_to_all | solution.py:264

commit v4 on v3

--- a/solution.py
+++ b/solution.py
@@ -173,6 +173,81 @@
     )
 
 
+def last_smear_kernel(blocks, d, idx_ref, field_ref, res_ref, _, out, bh, bl, pad, vh, vl, uh, ul):
+    rows = field_ref.shape[0]
+    per = blocks // 4
+    base = (idx_ref[0] ^ d) * per
+    flip = idx_ref[1] * (per // 2)
+    near = lax.broadcasted_iota(jnp.int32, (rows, LANES), 1) < LANES // 2
+    row = lax.broadcasted_iota(jnp.int32, (LANES, LANES), 0)
+    col = lax.broadcasted_iota(jnp.int32, (LANES, LANES), 1)
+    inside = jnp.abs(row - col) <= RADIUS
+    left, right = base > 0, base + per < blocks
+
+    def take(ref, j):
+        return ref[:, block(jnp.clip(j, 0, blocks - 1))]
+
+    def at(i):
+        return slice(i * LANES, (i + 1) * LANES)
+
+    def valid(i, margin, x):
+        if i < margin:
+            return jnp.where(left, x, 0.0)
+        return jnp.where(right, x, 0.0) if i >= per + margin else x
+
+    def window(ref, i):
+        return jnp.concatenate([ref[:, at(i)], jnp.where(near, ref[:, at(i + 1)], ref[:, at(i - 1)])], axis=1)
+
+    pad[...] = jnp.zeros(pad.shape, F32)
+
+    def bands(step, carry):
+        for u in range((per + 2) // 2):
+            i = step * ((per + 2) // 2) + u
+            j = base + i - 1
+            pad[u, 0:TAPS, :] = jnp.where((j >= 0) & (j < blocks), take(res_ref, j), 0.0)
+            band = pltpu.roll(jnp.transpose(pad[u]), LANES - RADIUS, 1, stride=1, stride_axis=0)
+            bh[block(i), 0:LANES], bl[block(i), 0:LANES] = split(jnp.where(inside, band, 0.0))
+            bh[block(i), LANES:], bl[block(i), LANES:] = split(jnp.where(inside, 0.0, band))
+        return carry
+
+    lax.fori_loop(0, 2, bands, 0)
+    for i in range(per + 4):
+        vh[:, at(i)], vl[:, at(i)] = split(valid(i, 2, take(field_ref, base + i - 2)))
+    for i in range(per + 2):
+        blurred = mm3((window(vh, i + 1), window(vl, i + 1)), (bh[at(i), :], bl[at(i), :]), NT)
+        uh[:, at(i)], ul[:, at(i)] = split(valid(i, 1, take(field_ref, base + i - 1) / blurred))
+
+    def stack(ref, i):
+        half = LANES // 2
+        after = ref[(i + 1) * LANES : (i + 1) * LANES + half, LANES:]
+        before = ref[(i - 1) * LANES + half : i * LANES, LANES:]
+        return jnp.concatenate([ref[at(i), 0:LANES], after, before], axis=0)
+
+    for i in range(per):
+        h, l = stack(bh, i + 1), stack(bl, i + 1)
+        total = mm3((window(uh, i + 1), window(ul, i + 1)), (h, l), NN)
+        weight = jnp.sum(h.astype(F32) + l.astype(F32), axis=0, keepdims=True)
+        out[:, block(i ^ flip)] = take(field_ref, base + i) * total / weight
+
+
+def last_smear(d, idx, field, resolution, token):
+    rows, width = field.shape
+    blocks = width // LANES
+    per = blocks // 4
+    scratch = [pltpu.VMEM(((per + 2) * LANES, 2 * LANES), BF16)] * 2
+    scratch += [pltpu.VMEM(((per + 2) // 2, LANES, LANES), F32)]
+    scratch += [pltpu.VMEM((rows, (per + 4) * LANES), BF16)] * 2 + [pltpu.VMEM((rows, (per + 2) * LANES), BF16)] * 2
+    return call(
+        functools.partial(last_smear_kernel, blocks, d),
+        [(rows, width // 4)],
+        [idx, field, resolution, token],
+        "smear",
+        1024,
+        scratch,
+        1,
+    )[0]
+
+
 def fold(x):
     return jnp.sum(jnp.sum(x.reshape(4, x.shape[0] // 32, 8, x.shape[1]), axis=1), axis=0)
 
@@ -269,12 +344,12 @@
     zi = lax.axis_index("z")
     comps = components_start.shape[0]
     idx = jnp.stack([xi, ci]).astype(jnp.int32)
+    xs = [None] * 4
     bh, bl = make_bands(resolution)
-    xs = [None] * 4
-    for d in (2, 1, 3, 0):
+    for d in (2, 1, 3):
         xs[d], zero, bh, bl = smear(d, idx, measured, bh, bl)
-        if d:
-            xs[d] = swap(xs[d], "x", d)
+        xs[d] = swap(xs[d], "x", d)
+    xs[0] = last_smear(0, idx, measured, resolution, zero)
     start = spread(components_start.T, "y", 4, zero[0, 0])
     half = start.shape[0] // 2
     mine = lax.dynamic_slice_in_dim(start, ci * half, half)

time: 226 us -> 226 us (level)
  waiting for transfers between devices: 52.7 us -> 48.5 us
    all_to_all x2, waiting for transfers between devices: 23.7 us -> 19.7 us  [spread(): return lax.all_to_all(y, axes, 0, 0).reshape((-1,) + x.shape[1:])]
    unnamed x8 -> x12, local copies, waits for them, and re-layouts: 4.4 us -> 6 us
where the time goes in v4:
time: 226 us; the launch traced here: 225 us
  blocking collectives  82.8 us (37%)
  waiting for transfers between devices  48.5 us (21%)
  starting transfers between devices  45.1 us (20%)
  Pallas kernels  32.8 us (15%)
  local copies, waits for them, and re-layouts  10.7 us (5%)
  other arithmetic  3.77 us (2%)
    all_to_all x3, blocking collectives, spread(): return lax.all_to_all(y, axes, 0, 0).reshape((-1,) + x.shape[1:])  48 us
    all_to_all x2, blocking collectives, local(): total = jnp.sum(lax.all_to_all(packed, ('z', 'y'), 0, 0), axis=0)[:, 0]  34.8 us
    pallas_call x34, Pallas kernels, call(): pl.pallas_call(kernel, out_shape=[jax.ShapeDtypeStruct(o, F32) for o in o...  30.4 us
    ppermute x24, starting transfers between devices, swap(): return lax.ppermute(x, axis, [(i, i ^ distance) for i in range(size)])  26.1 us
    all_to_all x2, waiting for transfers between devices, spread(): return lax.all_to_all(y, axes, 0, 0).reshape((-1,) + x.shape[1:])  19.7 us
    ppermute x24, waiting for transfers between devices, swap(): return lax.ppermute(x, axis, [(i, i ^ distance) for i in range(size)])  16 us
    all_to_all x1, waiting for transfers between devices, local(): total = jnp.sum(lax.all_to_all(packed, ('z', 'y'), 0, 0), axis=0)[:, 0]  12.9 us
    all_to_all x1, starting transfers between devices, local(): total = jnp.sum(lax.all_to_all(packed, ('z', 'y'), 0, 0), axis=0)[:, 0]  10.9 us
  transfers between devices with their start and end apart: 27, of which 21 were waited for; matrix products, arithmetic and copies ran while one was open for 2% of the time, Pallas kernels for 11%

profile of v4, /device:TPU:32, one launch (start us, length us, event | category | flops | bytes accessed | tf_op | source)
XLA Modules:
  0.0 225.0 jit_solution(2770421584832039541)
XLA Ops:
  0.6 1.1 copy-done.2
  1.7 2.3 %bands.1 = (bf16[4352,256]{1,0:T(8,128)(2,1)S(1)}, bf16[4352,256]{1,0:T(8,128)(2,1)S(1)}) custom-call(f32[33,4096]{1,0:T(8,128)S(1)} %copy-done.2), custom_call_target="tpu_custom_call" | custom-call | flops 1048576 | bytes 12582912 | tf_op jit(solution)/shard_map/bands/pallas_call | solution.py:99
  4.2 1.6 copy-done
  5.7 2.3 %smear.4 = (f32[128,1024]{1,0:T(8,128)S(1)}, f32[8,128]{1,0:T(8,128)}, bf16[4352,256]{1,0:T(8,128)(2,1)S(1)}, bf16[4352,256]{1,0:T(8,128)(2,1)S(1)}) custom-call(s32[2]{0:T(128)S(1)} %pad_add_fusion.idx_ref, f32[128,4096]{1,0:T(8,128)S(1)} %copy-done, bf16[4352,256]{1,0:T(8,128)(2,1)S(1)} %get-tuple-element.42.bh_ref, ...), custom_call_target="tpu_custom_call", output_to_operand_aliasing={{2}: (2, {}), {3}: (3, {})} | custom-call | flops 1024 | bytes 1024 | tf_op jit(solution)/shard_map/smear/pallas_call | solution.py:49
  8.0 3.0 %collective-permute-start.1 = (f32[128,1024]{1,0:T(8,128)S(1)}, f32[128,1024]{1,0:T(8,128)S(1)}, u32[]{:S(2)}, u32[]{:S(2)}) collective-permute-start(f32[128,1024]{1,0:T(8,128)S(1)} %get-tuple-element.50), channel_id=1, source_target_pairs={{0,8},{4,12},{8,0},{12,4},{1,9},{5,13},{9,1},{13,5},{2,10},{6,14},... | collective-permute-start | bytes 1572872 | tf_op jit(solution)/shard_map/ppermute | solution.py:334
  11.0 2.5 %smear.5 = (f32[128,1024]{1,0:T(8,128)}, f32[8,128]{1,0:T(8,128)}, bf16[4352,256]{1,0:T(8,128)(2,1)S(1)}, bf16[4352,256]{1,0:T(8,128)(2,1)S(1)}) custom-call(s32[2]{0:T(128)S(1)} %pad_add_fusion.idx_ref, f32[128,4096]{1,0:T(8,128)S(1)} %copy-done, bf16[4352,256]{1,0:T(8,128)(2,1)S(1)} %get-tuple-element.44.bh_ref, ...), custom_call_target="tpu_custom_call", output_to_operand_aliasing={{2}: (2, {}), {3}: (3, {})} | custom-call | flops 1024 | bytes 1024 | tf_op jit(solution)/shard_map/smear/pallas_call | solution.py:49
  14.2 2.6 %smear.6 = (f32[128,1024]{1,0:T(8,128)}, f32[8,128]{1,0:T(8,128)S(1)}, bf16[4352,256]{1,0:T(8,128)(2,1)S(1)}, bf16[4352,256]{1,0:T(8,128)(2,1)S(1)}) custom-call(s32[2]{0:T(128)S(1)} %pad_add_fusion.idx_ref, f32[128,4096]{1,0:T(8,128)S(1)} %copy-done, bf16[4352,256]{1,0:T(8,128)(2,1)S(1)} %get-tuple-element.46.bh_ref, ...), custom_call_target="tpu_custom_call", output_to_operand_aliasing={{2}: (2, {}), {3}: (3, {})} | custom-call | flops 1024 | bytes 1024 | tf_op jit(solution)/shard_map/smear/pallas_call | solution.py:49
  19.4 4.5 %all-to-all-start = ((f32[4,256,128]{2,1,0:T(8,128)}), f32[4,256,128]{2,1,0:T(8,128)}, u32[]{:S(2)}, u32[]{:S(2)}) async-start(f32[4,256,128]{2,1,0:T(8,128)} %broadcast_in_dim.16), calls=%async_computation | async-start | bytes 1048576 | tf_op jit(solution)/shard_map/all_to_all | solution.py:339
  23.9 1.6 copy-done.1
  25.5 2.4 %smear.7.x0.x = f32[128,1024]{1,0:T(8,128)S(1)} custom-call(s32[2]{0:T(128)S(1)} %pad_add_fusion.idx_ref, f32[128,4096]{1,0:T(8,128)S(1)} %copy-done.1, f32[33,4096]{1,0:T(8,128)S(1)} %copy-done.3, f32[8,128]{1,0:T(8,128)S(1)} %get-tuple-element.48._), custom_call_target="tpu_custom_call" | custom-call | flops 1024 | bytes 1024 | tf_op jit(solution)/shard_map/smear/pallas_call | solution.py:49
  27.9 1.0 constant_dynamic-slice_fusion.3
  28.8 4.1 %all-to-all-done = f32[4,256,128]{2,1,0:T(8,128)} async-done(((f32[4,256,128]{2,1,0:T(8,128)}), f32[4,256,128]{2,1,0:T(8,128)}, u32[]{:S(2)}, u32[]{:S(2)}) %all-to-all-start) | async-done | bytes 524320 | tf_op jit(solution)/shard_map/all_to_all | solution.py:339
  32.9 1.1 constant_dynamic-slice_fusion
  36.2 1.4 components_keep.3
  37.8 1.0 pad_maximum_fusion
  38.8 10.9 %all-to-all-start.1 = ((f32[32,17,1,128]{3,2,1,0:T(1,128)}), f32[32,17,1,128]{3,2,1,0:T(1,128)S(1)}, u32[]{:S(2)}, u32[]{:S(2)}) async-start(f32[32,17,1,128]{3,2,1,0:T(1,128)} %pad_maximum_fusion), calls=%async_computation.1 | async-start | bytes 557056 | tf_op jit(solution)/shard_map/all_to_all | solution.py:369
  49.7 12.9 %all-to-all-done.1 = f32[32,17,1,128]{3,2,1,0:T(1,128)S(1)} async-done(((f32[32,17,1,128]{3,2,1,0:T(1,128)}), f32[32,17,1,128]{3,2,1,0:T(1,128)S(1)}, u32[]{:S(2)}, u32[]{:S(2)}) %all-to-all-start.1) | async-done | bytes 278560 | tf_op jit(solution)/shard_map/all_to_all | solution.py:369
  63.6 16.0 %all_to_all.40 = f32[32,16,128]{2,1,0:T(8,128)S(1)} all-to-all(f32[32,16,128]{2,1,0:T(8,128)S(1)} %broadcast_in_dim.18), channel_id=1, replica_groups=mesh['z'=8,'c'=2,'x'=4,'y'=4] {'z','y'}, dimensions={0} | all-to-all | bytes 524288 | tf_op jit(solution)/shard_map/all_to_all | solution.py:339
  79.6 1.5 loadings_own.3
  81.6 2.4 %collective-permute-start.5 = (f32[136,128]{1,0:T(8,128)S(1)}, f32[136,128]{1,0:T(8,128)S(1)}, u32[]{:S(2)}, u32[]{:S(2)}) collective-permute-start(f32[136,128]{1,0:T(8,128)S(1)} %loadings_other.13), channel_id=1, source_target_pairs={{0,8},{4,12},{8,0},{12,4},{1,9},{5,13},{9,1},{13,5},{2,10},{6,14},... | collective-permute-start | bytes 208904 | tf_op jit(solution)/shard_map/ppermute | solution.py:334
  85.8 1.2 collective-permute-start.7
  87.8 1.2 collective-permute-done.6
  89.0 2.4 %collective-permute-done.7 = f32[136,128]{1,0:T(8,128)S(1)} collective-permute-done((f32[136,128]{1,0:T(8,128)S(1)}, f32[136,128]{1,0:T(8,128)S(1)}, u32[]{:S(2)}, u32[]{:S(2)}) %collective-permute-start.7) | collective-permute-done | bytes 69664 | tf_op jit(solution)/shard_map/ppermute | solution.py:334
  91.4 1.5 collective-permute-start.9
  93.5 2.1 collective-permute-start.10
  96.1 1.2 collective-permute-done.9.l2.l
  99.7 1.4 components_keep.4
  101.6 17.4 %all_to_all.41 = f32[32,17,1,128]{3,2,1,0:T(1,128)S(1)} all-to-all(f32[32,17,1,128]{3,2,1,0:T(1,128)S(1)} %pad_maximum_fusion.1), channel_id=1, replica_groups=mesh['z'=8,'c'=2,'x'=4,'y'=4] {'z','y'}, dimensions={0} | all-to-all | bytes 557056 | tf_op jit(solution)/shard_map/all_to_all | solution.py:369
  119.2 16.0 %all_to_all.42 = f32[32,16,128]{2,1,0:T(8,128)S(1)} all-to-all(f32[32,16,128]{2,1,0:T(8,128)S(1)} %broadcast_in_dim.20), channel_id=1, replica_groups=mesh['z'=8,'c'=2,'x'=4,'y'=4] {'z','y'}, dimensions={0} | all-to-all | bytes 524288 | tf_op jit(solution)/shard_map/all_to_all | solution.py:339
  135.2 1.5 loadings_own.4
  137.2 1.2 collective-permute-start.13
  139.0 2.1 collective-permute-start.14
  141.6 1.2 collective-permute-start.15
  144.3 2.9 %collective-permute-done.15 = f32[136,128]{1,0:T(8,128)S(1)} collective-permute-done((f32[136,128]{1,0:T(8,128)S(1)}, f32[136,128]{1,0:T(8,128)S(1)}, u32[]{:S(2)}, u32[]{:S(2)}) %collective-permute-start.15) | collective-permute-done | bytes 69664 | tf_op jit(solution)/shard_map/ppermute | solution.py:334
  147.5 1.8 collective-permute-start.16
  149.4 2.1 collective-permute-start.18
  151.9 1.2 collective-permute-done.17.l2.l
  155.5 1.4 components_keep.5
  157.4 17.4 %all_to_all.43 = f32[32,17,1,128]{3,2,1,0:T(1,128)S(1)} all-to-all(f32[32,17,1,128]{3,2,1,0:T(1,128)S(1)} %pad_maximum_fusion.2), channel_id=1, replica_groups=mesh['z'=8,'c'=2,'x'=4,'y'=4] {'z','y'}, dimensions={0} | all-to-all | bytes 557056 | tf_op jit(solution)/shard_map/all_to_all | solution.py:369
  175.0 16.0 %all_to_all.44 = f32[32,16,128]{2,1,0:T(8,128)S(1)} all-to-all(f32[32,16,128]{2,1,0:T(8,128)S(1)} %broadcast_in_dim.22), channel_id=1, replica_groups=mesh['z'=8,'c'=2,'x'=4,'y'=4] {'z','y'}, dimensions={0} | all-to-all | bytes 524288 | tf_op jit(solution)/shard_map/all_to_all | solution.py:339
  191.0 1.5 loadings_own.5
  194.5 2.2 collective-permute-start.22
  197.2 1.3 collective-permute-start.23
  200.1 2.6 %collective-permute-done.23 = f32[136,128]{1,0:T(8,128)S(1)} collective-permute-done((f32[136,128]{1,0:T(8,128)S(1)}, f32[136,128]{1,0:T(8,128)S(1)}, u32[]{:S(2)}, u32[]{:S(2)}) %collective-permute-start.23) | collective-permute-done | bytes 69664 | tf_op jit(solution)/shard_map/ppermute | solution.py:334
  202.8 1.1 broadcast_in_dim.23
  203.9 3.7 %all-to-all-start.7 = ((f32[16,128,128]{2,1,0:T(8,128)}), f32[16,128,128]{2,1,0:T(8,128)S(1)}, u32[]{:S(2)}, u32[]{:S(2)}) async-start(f32[16,128,128]{2,1,0:T(8,128)} %broadcast_in_dim.23), calls=%async_computation.7 | async-start | bytes 2097152 | tf_op jit(solution)/shard_map/all_to_all | solution.py:339
  208.4 15.6 %all-to-all-done.7 = f32[16,128,128]{2,1,0:T(8,128)S(1)} async-done(((f32[16,128,128]{2,1,0:T(8,128)}), f32[16,128,128]{2,1,0:T(8,128)S(1)}, u32[]{:S(2)}, u32[]{:S(2)}) %all-to-all-start.7) | async-done | bytes 1048608 | tf_op jit(solution)/shard_map/all_to_all | solution.py:339
  224.0 1.0 copy.26
  (103 shorter events, 25.8 us)
Async XLA Ops:
  0.6 1.1 copy-start.2
  4.2 1.6 copy-start
  8.0 26.5 %collective-permute-start.1 = (f32[128,1024]{1,0:T(8,128)S(1)}, f32[128,1024]{1,0:T(8,128)S(1)}, u32[]{:S(2)}, u32[]{:S(2)}) collective-permute-start(f32[128,1024]{1,0:T(8,128)S(1)} %get-tuple-element.50), channel_id=1, source_target_pairs={{0,8},{4,12},{8,0},{12,4},{1,9},{5,13},{9,1},{13,5},{2,10},{6,14},... | collective-permute-start | bytes 1572872 | tf_op jit(solution)/shard_map/ppermute | solution.py:334
  13.6 21.4 %collective-permute-start = (f32[128,1024]{1,0:T(8,128)}, f32[128,1024]{1,0:T(8,128)S(1)}, u32[]{:S(2)}, u32[]{:S(2)}) collective-permute-start(f32[128,1024]{1,0:T(8,128)} %get-tuple-element.49), channel_id=1, source_target_pairs={{0,4},{4,0},{8,12},{12,8},{1,5},{5,1},{9,13},{13,9},{2,6},{6,2},{1... | collective-permute-start | bytes 1572872 | tf_op jit(solution)/shard_map/ppermute | solution.py:334
  14.2 3.6 %copy-start.4 = (f32[128,256]{1,0:T(8,128)S(1)}, f32[128,256]{1,0:T(8,128)}, u32[]{:S(2)}) copy-start(f32[128,256]{1,0:T(8,128)} %param.7) | copy-start | bytes 393220
  16.7 7.2 %copy-start.3 = (f32[33,4096]{1,0:T(8,128)S(1)}, f32[33,4096]{1,0:T(8,128)}, u32[]{:S(2)}) copy-start(f32[33,4096]{1,0:T(8,128)} %res_ref.3) | copy-start | bytes 1622020
  16.7 18.8 %collective-permute-start.2 = (f32[128,1024]{1,0:T(8,128)}, f32[128,1024]{1,0:T(8,128)S(1)}, u32[]{:S(2)}, u32[]{:S(2)}) collective-permute-start(f32[128,1024]{1,0:T(8,128)} %get-tuple-element.51), channel_id=1, source_target_pairs={{0,12},{4,8},{8,4},{12,0},{1,13},{5,9},{9,5},{13,1},{2,14},{6,10},... | collective-permute-start | bytes 1572872 | tf_op jit(solution)/shard_map/ppermute | solution.py:334
  19.4 13.5 %all-to-all-start = ((f32[4,256,128]{2,1,0:T(8,128)}), f32[4,256,128]{2,1,0:T(8,128)}, u32[]{:S(2)}, u32[]{:S(2)}) async-start(f32[4,256,128]{2,1,0:T(8,128)} %broadcast_in_dim.16), calls=%async_computation | async-start | bytes 1048576 | tf_op jit(solution)/shard_map/all_to_all | solution.py:339
  23.9 1.6 copy-start.1
  36.1 1.6 collective-permute-start.3
  38.8 23.9 %all-to-all-start.1 = ((f32[32,17,1,128]{3,2,1,0:T(1,128)}), f32[32,17,1,128]{3,2,1,0:T(1,128)S(1)}, u32[]{:S(2)}, u32[]{:S(2)}) async-start(f32[32,17,1,128]{3,2,1,0:T(1,128)} %pad_maximum_fusion), calls=%async_computation.1 | async-start | bytes 557056 | tf_op jit(solution)/shard_map/all_to_all | solution.py:369
  79.6 1.5 collective-permute-start.4
  81.6 6.2 %collective-permute-start.5 = (f32[136,128]{1,0:T(8,128)S(1)}, f32[136,128]{1,0:T(8,128)S(1)}, u32[]{:S(2)}, u32[]{:S(2)}) collective-permute-start(f32[136,128]{1,0:T(8,128)S(1)} %loadings_other.13), channel_id=1, source_target_pairs={{0,8},{4,12},{8,0},{12,4},{1,9},{5,13},{9,1},{13,5},{2,10},{6,14},... | collective-permute-start | bytes 208904 | tf_op jit(solution)/shard_map/ppermute | solution.py:334
  84.6 4.4 %collective-permute-start.6 = (f32[136,128]{1,0:T(8,128)S(1)}, f32[136,128]{1,0:T(8,128)S(1)}, u32[]{:S(2)}, u32[]{:S(2)}) collective-permute-start(f32[136,128]{1,0:T(8,128)S(1)} %loadings_other.14), channel_id=1, source_target_pairs={{0,4},{4,0},{8,12},{12,8},{1,5},{5,1},{9,13},{13,9},{2,6},{6,2},{1... | collective-permute-start | bytes 208904 | tf_op jit(solution)/shard_map/ppermute | solution.py:334
  85.8 5.6 %collective-permute-start.7 = (f32[136,128]{1,0:T(8,128)S(1)}, f32[136,128]{1,0:T(8,128)S(1)}, u32[]{:S(2)}, u32[]{:S(2)}) collective-permute-start(f32[136,128]{1,0:T(8,128)S(1)} %loadings_other.15), channel_id=1, source_target_pairs={{0,12},{4,8},{8,4},{12,0},{1,13},{5,9},{9,5},{13,1},{2,14},{6,10},... | collective-permute-start | bytes 208904 | tf_op jit(solution)/shard_map/ppermute | solution.py:334
  91.4 5.9 %collective-permute-start.9 = (f32[128,128]{1,0:T(8,128)S(1)}, f32[128,128]{1,0:T(8,128)S(1)}, u32[]{:S(2)}, u32[]{:S(2)}) collective-permute-start(f32[128,128]{1,0:T(8,128)S(1)} %fusion.2.l0.l), channel_id=1, source_target_pairs={{0,8},{4,12},{8,0},{12,4},{1,9},{5,13},{9,1},{13,5},{2,10},{6,14},... | collective-permute-start | bytes 196616 | tf_op jit(solution)/shard_map/ppermute | solution.py:334
  92.9 4.9 %collective-permute-start.8 = (f32[128,128]{1,0:T(8,128)S(1)}, f32[128,128]{1,0:T(8,128)S(1)}, u32[]{:S(2)}, u32[]{:S(2)}) collective-permute-start(f32[128,128]{1,0:T(8,128)S(1)} %fusion.2.l0.l), channel_id=1, source_target_pairs={{0,4},{4,0},{8,12},{12,8},{1,5},{5,1},{9,13},{13,9},{2,6},{6,2},{1... | collective-permute-start | bytes 196616 | tf_op jit(solution)/shard_map/ppermute | solution.py:334
  93.5 5.5 %collective-permute-start.10 = (f32[128,128]{1,0:T(8,128)S(1)}, f32[128,128]{1,0:T(8,128)S(1)}, u32[]{:S(2)}, u32[]{:S(2)}) collective-permute-start(f32[128,128]{1,0:T(8,128)S(1)} %fusion.2.l0.l), channel_id=1, source_target_pairs={{0,12},{4,8},{8,4},{12,0},{1,13},{5,9},{9,5},{13,1},{2,14},{6,10},... | collective-permute-start | bytes 196616 | tf_op jit(solution)/shard_map/ppermute | solution.py:334
  99.6 1.6 collective-permute-start.11
  135.2 1.5 collective-permute-start.12
  137.2 6.3 %collective-permute-start.13 = (f32[136,128]{1,0:T(8,128)S(1)}, f32[136,128]{1,0:T(8,128)S(1)}, u32[]{:S(2)}, u32[]{:S(2)}) collective-permute-start(f32[136,128]{1,0:T(8,128)S(1)} %loadings_other.17), channel_id=1, source_target_pairs={{0,8},{4,12},{8,0},{12,4},{1,9},{5,13},{9,1},{13,5},{2,10},{6,14},... | collective-permute-start | bytes 208904 | tf_op jit(solution)/shard_map/ppermute | solution.py:334
  139.0 5.3 %collective-permute-start.14 = (f32[136,128]{1,0:T(8,128)S(1)}, f32[136,128]{1,0:T(8,128)S(1)}, u32[]{:S(2)}, u32[]{:S(2)}) collective-permute-start(f32[136,128]{1,0:T(8,128)S(1)} %loadings_other.18), channel_id=1, source_target_pairs={{0,4},{4,0},{8,12},{12,8},{1,5},{5,1},{9,13},{13,9},{2,6},{6,2},{1... | collective-permute-start | bytes 208904 | tf_op jit(solution)/shard_map/ppermute | solution.py:334
  141.6 5.6 %collective-permute-start.15 = (f32[136,128]{1,0:T(8,128)S(1)}, f32[136,128]{1,0:T(8,128)S(1)}, u32[]{:S(2)}, u32[]{:S(2)}) collective-permute-start(f32[136,128]{1,0:T(8,128)S(1)} %loadings_other.19), channel_id=1, source_target_pairs={{0,12},{4,8},{8,4},{12,0},{1,13},{5,9},{9,5},{13,1},{2,14},{6,10},... | collective-permute-start | bytes 208904 | tf_op jit(solution)/shard_map/ppermute | solution.py:334
  147.3 5.9 %collective-permute-start.17 = (f32[128,128]{1,0:T(8,128)S(1)}, f32[128,128]{1,0:T(8,128)S(1)}, u32[]{:S(2)}, u32[]{:S(2)}) collective-permute-start(f32[128,128]{1,0:T(8,128)S(1)} %fusion.1.l0.l), channel_id=1, source_target_pairs={{0,8},{4,12},{8,0},{12,4},{1,9},{5,13},{9,1},{13,5},{2,10},{6,14},... | collective-permute-start | bytes 196616 | tf_op jit(solution)/shard_map/ppermute | solution.py:334
  147.5 6.1 %collective-permute-start.16 = (f32[128,128]{1,0:T(8,128)S(1)}, f32[128,128]{1,0:T(8,128)S(1)}, u32[]{:S(2)}, u32[]{:S(2)}) collective-permute-start(f32[128,128]{1,0:T(8,128)S(1)} %fusion.1.l0.l), channel_id=1, source_target_pairs={{0,4},{4,0},{8,12},{12,8},{1,5},{5,1},{9,13},{13,9},{2,6},{6,2},{1... | collective-permute-start | bytes 196616 | tf_op jit(solution)/shard_map/ppermute | solution.py:334
  149.4 5.5 %collective-permute-start.18 = (f32[128,128]{1,0:T(8,128)S(1)}, f32[128,128]{1,0:T(8,128)S(1)}, u32[]{:S(2)}, u32[]{:S(2)}) collective-permute-start(f32[128,128]{1,0:T(8,128)S(1)} %fusion.1.l0.l), channel_id=1, source_target_pairs={{0,12},{4,8},{8,4},{12,0},{1,13},{5,9},{9,5},{13,1},{2,14},{6,10},... | collective-permute-start | bytes 196616 | tf_op jit(solution)/shard_map/ppermute | solution.py:334
  155.4 1.6 collective-permute-start.19
  191.0 1.5 collective-permute-start.20
  193.1 6.6 %collective-permute-start.21 = (f32[136,128]{1,0:T(8,128)S(1)}, f32[136,128]{1,0:T(8,128)S(1)}, u32[]{:S(2)}, u32[]{:S(2)}) collective-permute-start(f32[136,128]{1,0:T(8,128)S(1)} %loadings_other.21), channel_id=1, source_target_pairs={{0,8},{4,12},{8,0},{12,4},{1,9},{5,13},{9,1},{13,5},{2,10},{6,14},... | collective-permute-start | bytes 208904 | tf_op jit(solution)/shard_map/ppermute | solution.py:334
  194.5 5.6 %collective-permute-start.22 = (f32[136,128]{1,0:T(8,128)S(1)}, f32[136,128]{1,0:T(8,128)S(1)}, u32[]{:S(2)}, u32[]{:S(2)}) collective-permute-start(f32[136,128]{1,0:T(8,128)S(1)} %loadings_other.22), channel_id=1, source_target_pairs={{0,4},{4,0},{8,12},{12,8},{1,5},{5,1},{9,13},{13,9},{2,6},{6,2},{1... | collective-permute-start | bytes 208904 | tf_op jit(solution)/shard_map/ppermute | solution.py:334
  197.2 5.6 %collective-permute-start.23 = (f32[136,128]{1,0:T(8,128)S(1)}, f32[136,128]{1,0:T(8,128)S(1)}, u32[]{:S(2)}, u32[]{:S(2)}) collective-permute-start(f32[136,128]{1,0:T(8,128)S(1)} %loadings_other.23), channel_id=1, source_target_pairs={{0,12},{4,8},{8,4},{12,0},{1,13},{5,9},{9,5},{13,1},{2,14},{6,10},... | collective-permute-start | bytes 208904 | tf_op jit(solution)/shard_map/ppermute | solution.py:334
  203.9 20.1 %all-to-all-start.7 = ((f32[16,128,128]{2,1,0:T(8,128)}), f32[16,128,128]{2,1,0:T(8,128)S(1)}, u32[]{:S(2)}, u32[]{:S(2)}) async-start(f32[16,128,128]{2,1,0:T(8,128)} %broadcast_in_dim.23), calls=%async_computation.7 | async-start | bytes 2097152 | tf_op jit(solution)/shard_map/all_to_all | solution.py:339
